TPU v7x, 512 devices: a whole 4x8x8 slice. The times are simulated.
512 devices in a mesh: row: 2 (over core), circ: 32 (over z, x), ax: 8 (over y).
Axes of the slice: x: 4, y: 8, z: 8, core: 2. Of those that a mesh axis runs over, the one named last changes fastest.
Arguments:
- state: float32 [2, 5, 128, 1024, 128], P('row', None, 'ax', 'circ'), may hold values from -6 to 42, as said below
- rotor_step: int32 [1], replicated, may hold values from 0 to 99999
Outputs:
- advanced: float32 [2, 5, 128, 1024, 128], P('row', None, 'ax', 'circ')
- coupled_modes: float32 [2, 128, 5, 2, 128], P('row', 'circ', None, None, 'ax')
Inputs may be any that keep to these rules, and one draw needn't show every extreme that they name: Density lies in 0.7 to 1.3 and the pressure the state implies in 0.5 to 1.7. `rotor_step`: circumferential pitches the rotor has turned.
All inputs are finite; a program needn't handle non-finite values.
Results may differ from a plain program's by a relative error of at most 0.000082.
Values sent between devices are 32-bit elements; how exact they have to be, the bound alone decides.
A program may use at most 192 MiB of HBM per device.

v0:
```python
import math

import jax
import jax.numpy as jnp
from jax import lax
from jax.sharding import PartitionSpec as P

MODES = 128


courant = 0.8
two_pi = 2.0 * math.pi


def swapped(value, axis, bit):
    mask = 2**bit
    pairs = [(source, source ^ mask) for source in range(lax.axis_size(axis))]
    return lax.ppermute(value, axis, pairs)


def with_halo(cells, sides, width, closed):
    for axis, dim in sides:
        count = lax.axis_size(axis)
        ends = count if closed else count - 1
        head = lax.slice_in_dim(cells, 0, width, axis=dim)
        tail = lax.slice_in_dim(cells, cells.shape[dim] - width, cells.shape[dim], axis=dim)
        cells = jnp.concatenate(
            [
                lax.ppermute(tail, axis, [(i, (i + 1) % count) for i in range(ends)]),
                cells,
                lax.ppermute(head, axis, [((i + 1) % count, i) for i in range(ends)]),
            ],
            axis=dim,
        )
    return cells


def spread(shard, axis, root):
    mine = lax.axis_index(axis) == root
    return lax.psum(jnp.where(mine, shard, jnp.zeros_like(shard)), axis)


def primitive(state):
    density = state[0]
    vel_axial = state[1] / density
    vel_circ = state[2] / density
    vel_radial = state[3] / density
    pressure = 0.4 * (
        state[4] - 0.5 * (state[1] * vel_axial + state[2] * vel_circ + state[3] * vel_radial)
    )
    return (density, (vel_axial, vel_circ, vel_radial), pressure)


def fluxes(state, direction):
    density, velocity, pressure = primitive(state)
    moving = velocity[direction]
    components = [
        state[0] * moving,
        state[1] * moving,
        state[2] * moving,
        state[3] * moving,
        state[4] * moving + pressure * moving,
    ]
    components[1 + direction] = components[1 + direction] + pressure
    return jnp.stack(components)


def wave_speed(state):
    density, velocity, pressure = primitive(state)
    sound_speed = jnp.sqrt(1.4 * pressure / density)
    fastest = jnp.maximum(
        jnp.maximum(jnp.abs(velocity[0]), jnp.abs(velocity[1])), jnp.abs(velocity[2])
    )
    return jnp.max(fastest + sound_speed)


def advance(state, axial_ext, axial_flux, circ_ext, circ_flux, speed_max):
    radial_ext = jnp.concatenate([state[..., :1], state, state[..., -1:]], axis=3)
    radial_flux = fluxes(radial_ext, 2)
    convection = (axial_flux[:, 2:] - axial_flux[:, :-2]) * 0.5
    convection = convection + (circ_flux[:, :, 2:] - circ_flux[:, :, :-2]) * 0.5
    convection = convection + (radial_flux[..., 2:] - radial_flux[..., :-2]) * 0.5
    smoothing = axial_ext[:, 2:] - 2.0 * state + axial_ext[:, :-2]
    smoothing = smoothing + (circ_ext[:, :, 2:] - 2.0 * state + circ_ext[:, :, :-2])
    smoothing = smoothing + (radial_ext[..., 2:] - 2.0 * state + radial_ext[..., :-2])
    time_step = courant / (3.0 * speed_max)
    return state - time_step * convection + courant / 6.0 * smoothing


def basis(mode_count, cell_first, cell_count, total_cells):
    mode_index = lax.iota(jnp.int32, mode_count)
    cell_index = cell_first + lax.iota(jnp.int32, cell_count)
    phase_index = mode_index[:, None] * cell_index[None, :] % total_cells
    angles = phase_index.astype(jnp.float32) * (two_pi / total_cells)
    norm_scale = math.sqrt(2.0 / total_cells)
    return (jnp.cos(angles) * norm_scale, -jnp.sin(angles) * norm_scale)


def project(interface, cosines, sines):
    real_part = jnp.einsum("mj,fjr->mfr", cosines, interface, precision=lax.Precision.HIGHEST)
    imag_part = jnp.einsum("mj,fjr->mfr", sines, interface, precision=lax.Precision.HIGHEST)
    return jnp.stack([real_part, imag_part], axis=2)


def rotate(coeffs, mode_first, rotor_step, orient, total_cells):
    mode_index = mode_first + lax.iota(jnp.int32, coeffs.shape[0])
    phase_index = mode_index * rotor_step[0] % total_cells
    angles = phase_index.astype(jnp.float32) * (two_pi / total_cells)
    cosine = jnp.cos(angles)[:, None, None]
    sine_part = jnp.sin(angles)[:, None, None]
    real_part = coeffs[:, :, 0]
    imag_part = coeffs[:, :, 1]
    new_real = real_part * cosine - orient * imag_part * sine_part
    new_imag = orient * real_part * sine_part + imag_part * cosine
    return jnp.stack([new_real, new_imag], axis=2)


def edge_fix(extended, inner):
    position = lax.axis_index("ax")
    last_index = lax.axis_size("ax") - 1
    lower_ghost = jnp.where(position == 0, inner[:, :1], extended[:, :1])
    upper_ghost = jnp.where(position == last_index, inner[:, -1:], extended[:, -1:])
    return jnp.concatenate([lower_ghost, extended[:, 1:-1], upper_ghost], axis=1)


def transformed(interface, total_cells):
    cells_here = interface.shape[1]
    first_cell = lax.axis_index("circ") * cells_here
    local_modes = MODES // lax.axis_size("circ")
    cosines, sines = basis(lax.axis_size("circ") * local_modes, first_cell, cells_here, total_cells)
    return lax.psum_scatter(
        project(interface, cosines, sines), "circ", scatter_dimension=0, tiled=True
    )


def crossed(coeffs, rotor_step, orient, total_cells):
    mode_first = lax.axis_index("circ") * coeffs.shape[0]
    turned = rotate(coeffs, mode_first, rotor_step, orient, total_cells)
    return swapped(turned, "row", 0)


def on_device(state, rotor_step):
    current = state[0]
    radial = current.shape[3]
    total_cells = current.shape[2] * lax.axis_size("circ")
    speed_max = lax.pmax(wave_speed(current), ("row", "circ", "ax"))
    axial_ext = edge_fix(with_halo(current, (("ax", 1),), 1, False), current)
    axial_flux = fluxes(axial_ext, 0)
    circ_ext = with_halo(current, (("circ", 2),), 1, True)
    circ_flux = fluxes(circ_ext, 1)
    updated = advance(current, axial_ext, axial_flux, circ_ext, circ_flux, speed_max)
    interface = updated[:, -1]
    orient = 1.0 - 2.0 * lax.axis_index("row").astype(jnp.float32)
    band_width = radial // lax.axis_size("ax")
    band_first = lax.axis_index("ax") * band_width
    coeffs = crossed(transformed(interface, total_cells), rotor_step, orient, total_cells)
    shared_modes = spread(coeffs, "ax", lax.axis_size("ax") - 1)
    result = lax.dynamic_slice_in_dim(shared_modes, band_first, band_width, 3)
    return (updated[None], result[None])


def solution(mesh):
    placed = (P("row", None, "ax", "circ", None), P())
    return jax.shard_map(
        on_device,
        mesh=mesh,
        in_specs=placed,
        out_specs=(P("row", None, "ax", "circ", None), P("row", "circ", None, None, "ax")),
        check_vma=False,
    )
```

profile of v0, /device:TPU:1, one launch (start us, length us, event | category | flops | bytes accessed | tf_op | source)
XLA Modules:
  0.0 336.4 jit_solution(17847131112099256268)
XLA Ops:
  7.2 1.4 copy.16
  8.6 0.7 fusion.72
  9.3 3.9 %collective-permute-start.2 = (f32[5,16,1,128]{3,2,0,1:T(1,128)}, f32[5,16,1,128]{3,2,0,1:T(1,128)S(1)}, u32[]{:S(2)}, u32[]{:S(2)}) collective-permute-start(f32[5,16,1,128]{3,2,0,1:T(1,128)} %get-tuple-element.25), channel_id=1, source_target_pairs={{0,8},{8,16},{16,24},{24,32},{32,40},{40,48},{48,56},{56,64},{64,7... | collective-permute-start | bytes 122888 | tf_op jit(solution)/shard_map/ppermute | solution.py:29
  13.3 11.7 %collective-permute-start.3 = (f32[5,16,1,128]{3,2,0,1:T(1,128)}, f32[5,16,1,128]{3,2,0,1:T(1,128)S(1)}, u32[]{:S(2)}, u32[]{:S(2)}) collective-permute-start(f32[5,16,1,128]{3,2,0,1:T(1,128)} %get-tuple-element.24), channel_id=1, source_target_pairs={{8,0},{16,8},{24,16},{32,24},{40,32},{48,40},{56,48},{64,56},{72,6... | collective-permute-start | bytes 122888 | tf_op jit(solution)/shard_map/ppermute | solution.py:31
  25.0 1.3 collective-permute-start.1
  26.3 4.1 %collective-permute-start = (f32[5,1,32,128]{3,2,0,1:T(8,128)S(1)}, f32[5,1,32,128]{3,2,0,1:T(8,128)S(1)}, u32[]{:S(2)}, u32[]{:S(2)}) collective-permute-start(f32[5,1,32,128]{3,2,0,1:T(8,128)S(1)} %get-tuple-element.23), channel_id=1, source_target_pairs={{0,1},{1,2},{2,3},{3,4},{4,5},{5,6},{6,7},{8,9},{9,10},{10,11},{11... | collective-permute-start | bytes 245768 | tf_op jit(solution)/shard_map/ppermute | solution.py:29
  30.4 0.5 fusion.73
  30.9 0.9 fusion.35
  31.8 1.2 pad_maximum_fusion
  33.0 1.1 multiply_dynamic-update-slice_fusion.3
  34.1 0.9 multiply_dynamic-update-slice_fusion.2
  35.0 0.9 multiply_dynamic-update-slice_fusion.1
  35.9 1.4 add_dynamic-update-slice_fusion
  37.3 2.2 multiply_dynamic-update-slice_fusion
  39.5 96.4 %pmax.7 = f32[]{:T(128)} all-reduce(f32[]{:T(128)} %fusion.35), channel_id=1, replica_groups=mesh['row'=2,'circ'=32,'ax'=8] {'row','circ','ax'}, use_global_device_ids=true, to_apply=%region_1.0 | all-reduce | flops 1 | bytes 8 | tf_op jit(solution)/shard_map/pmax | solution.py:146
  136.6 0.3 pad_maximum_fusion.1
  137.0 0.2 add_dynamic-update-slice_fusion.1
  137.3 0.1 pad_maximum_fusion.2
  137.5 0.2 add_dynamic-update-slice_fusion.2
  137.9 1.1 copy-done.2
  139.1 3.8 %fusion.3 = f32[5,16,32,128]{3,2,0,1:T(8,128)S(1)} fusion(f32[5,16,32,128]{3,2,0,1:T(8,128)S(1)} %bitcast.91, f32[5,16,32,1]{3,2,0,1:T(8,128)S(1)} %copy-done.2, f32[5,16,32,1]{3,2,0,1:T(8,128)S(1)} %get-tuple-element.26, f32[5,16,1,128]{3,2,0,1:T(1,128)S(1)} %collective-permute-done.2, f32[5,16,1,128]{3,2,0,1:T(1,128)S(1)} %collective-permute-done.3, ...), kind=kLoop, calls=%fused_computation.7 | loop fusion | flops 7864320 | bytes 10752004 | tf_op jit(solution)/shard_map/add | solution.py:87
  142.9 0.6 convolution_bitcast_fusion
  143.5 0.4 copy-done.3
  143.9 0.6 convolution_bitcast_fusion.1
  144.5 0.9 pad_maximum_fusion.9
  146.1 1.3 dynamic-slice
  148.1 149.2 %all-reduce.3.cloned.1.call-done = f32[128,5,2,128]{3,0,1,2:T(8,128)} async-done(((f32[128,5,2,128]{3,0,1,2:T(8,128)}), f32[128,5,2,128]{3,0,1,2:T(8,128)}) %all-reduce.3.cloned.1.call-update) | async-done | bytes 655376
  297.3 0.8 multiply_subtract_fusion.1
  298.1 7.1 %collective-permute-start.4 = (f32[4,5,2,128]{3,0,1,2:T(4,128)S(1)}, f32[4,5,2,128]{3,0,1,2:T(4,128)S(1)}, u32[]{:S(2)}, u32[]{:S(2)}) collective-permute-start(f32[4,5,2,128]{3,0,1,2:T(4,128)S(1)} %pad_maximum_fusion.10), channel_id=1, source_target_pairs={{0,256},{256,0},{1,257},{257,1},{2,258},{258,2},{3,259},{259,3},{4... | collective-permute-start | bytes 61448 | tf_op jit(solution)/shard_map/ppermute | solution.py:18
  305.2 1.2 copy.11
  306.4 22.5 %psum.7 = f32[4,5,2,128]{3,0,1,2:T(4,128)S(1)} all-reduce(f32[4,5,2,128]{3,0,1,2:T(4,128)S(1)} %broadcast_select_fusion.2), channel_id=1, replica_groups=mesh['row'=2,'circ'=32,'ax'=8] {'ax'}, use_global_device_ids=true, to_apply=%region_3.4 | all-reduce | flops 5120 | bytes 40960 | tf_op jit(solution)/shard_map/psum | solution.py:40
  329.0 0.6 copy.17
  (32 shorter events, 0.7 us)
Async XLA Ops:
  7.2 290.1 %all-reduce.3.cloned.1.call-start = ((), (), s32[]{:S(2)}) async-start(), calls=%async_computation | async-start | bytes 1310720
  9.3 127.3 %collective-permute-start.2 = (f32[5,16,1,128]{3,2,0,1:T(1,128)}, f32[5,16,1,128]{3,2,0,1:T(1,128)S(1)}, u32[]{:S(2)}, u32[]{:S(2)}) collective-permute-start(f32[5,16,1,128]{3,2,0,1:T(1,128)} %get-tuple-element.25), channel_id=1, source_target_pairs={{0,8},{8,16},{16,24},{24,32},{32,40},{40,48},{48,56},{56,64},{64,7... | collective-permute-start | bytes 122888 | tf_op jit(solution)/shard_map/ppermute | solution.py:29
  13.3 123.4 %collective-permute-start.3 = (f32[5,16,1,128]{3,2,0,1:T(1,128)}, f32[5,16,1,128]{3,2,0,1:T(1,128)S(1)}, u32[]{:S(2)}, u32[]{:S(2)}) collective-permute-start(f32[5,16,1,128]{3,2,0,1:T(1,128)} %get-tuple-element.24), channel_id=1, source_target_pairs={{8,0},{16,8},{24,16},{32,24},{40,32},{48,40},{56,48},{64,56},{72,6... | collective-permute-start | bytes 122888 | tf_op jit(solution)/shard_map/ppermute | solution.py:31
  25.0 112.3 %collective-permute-start.1 = (f32[5,1,32,128]{3,2,0,1:T(8,128)S(1)}, f32[5,1,32,128]{3,2,0,1:T(8,128)S(1)}, u32[]{:S(2)}, u32[]{:S(2)}) collective-permute-start(f32[5,1,32,128]{3,2,0,1:T(8,128)S(1)} %get-tuple-element.22), channel_id=1, source_target_pairs={{1,0},{2,1},{3,2},{4,3},{5,4},{6,5},{7,6},{9,8},{10,9},{11,10},{12... | collective-permute-start | bytes 245768 | tf_op jit(solution)/shard_map/ppermute | solution.py:31
  26.3 4.6 %copy-start.5 = (f32[1,5,16,32,128]{4,3,2,1,0:T(8,128)S(1)}, f32[1,5,16,32,128]{4,3,2,1,0:T(8,128)}, u32[]{:S(2)}) copy-start(f32[1,5,16,32,128]{4,3,2,1,0:T(8,128)} %param.2) | copy-start | bytes 3932164
  26.3 111.0 %collective-permute-start = (f32[5,1,32,128]{3,2,0,1:T(8,128)S(1)}, f32[5,1,32,128]{3,2,0,1:T(8,128)S(1)}, u32[]{:S(2)}, u32[]{:S(2)}) collective-permute-start(f32[5,1,32,128]{3,2,0,1:T(8,128)S(1)} %get-tuple-element.23), channel_id=1, source_target_pairs={{0,1},{1,2},{2,3},{3,4},{4,5},{5,6},{6,7},{8,9},{9,10},{10,11},{11... | collective-permute-start | bytes 245768 | tf_op jit(solution)/shard_map/ppermute | solution.py:29
  30.9 2.2 copy-start.1
  33.0 2.9 copy-start
  137.7 1.3 copy-start.2
  142.9 1.1 copy-start.3
  144.5 160.7 %copy-start.4 = (f32[5,16,32,128]{3,2,0,1:T(8,128)S(1)}, f32[5,16,32,128]{3,2,0,1:T(8,128)}, u32[]{:S(2)}) copy-start(f32[5,16,32,128]{3,2,0,1:T(8,128)} %copy-done.3) | copy-start | bytes 3932164
  298.1 8.3 %collective-permute-start.4 = (f32[4,5,2,128]{3,0,1,2:T(4,128)S(1)}, f32[4,5,2,128]{3,0,1,2:T(4,128)S(1)}, u32[]{:S(2)}, u32[]{:S(2)}) collective-permute-start(f32[4,5,2,128]{3,0,1,2:T(4,128)S(1)} %pad_maximum_fusion.10), channel_id=1, source_target_pairs={{0,256},{256,0},{1,257},{257,1},{2,258},{258,2},{3,259},{259,3},{4... | collective-permute-start | bytes 61448 | tf_op jit(solution)/shard_map/ppermute | solution.py:18
Sparse Core Ops, SparseCore 0:
  145.6 151.6 all-reduce.2
where the time goes:
time: 341 us; the launch traced here: 336 us
  waiting for transfers between devices  149 us (44%)
  blocking collectives  119 us (35%)
  starting transfers between devices  28.1 us (8%)
  between operations  16.3 us (5%)
  other arithmetic  15.3 us (4%)
  local copies, waits for them, and re-layouts  7.32 us (2%)
    unnamed x2, waiting for transfers between devices  149 us
    pmax x1, blocking collectives, on_device(): speed_max = lax.pmax(wave_speed(current), ('row', 'circ', 'ax'))  96.4 us
    psum x1, blocking collectives, spread(): return lax.psum(jnp.where(mine, shard, jnp.zeros_like(shard)), axis)  22.5 us
    ppermute x2, starting transfers between devices, with_halo(): lax.ppermute(head, axis, [((i + 1) % count, i) for i in range(ends)])  13 us
    ppermute x2, starting transfers between devices, with_halo(): lax.ppermute(tail, axis, [(i, (i + 1) % count) for i in range(ends)])  8.06 us
    ppermute x1, starting transfers between devices, swapped(): return lax.ppermute(value, axis, pairs)  7.07 us
  transfers between devices with their start and end apart: 6, of which 1 were waited for; matrix products, arithmetic and copies ran while one was open for 4% of the time, Pallas kernels for 0%

commit v1 on v0

v1 whole, which is shorter than its diff:
```python
import functools
import math

import jax
import jax.numpy as jnp
import numpy as np
from jax import lax
from jax.experimental import pallas as pl
from jax.experimental.pallas import tpu as pltpu
from jax.sharding import PartitionSpec as P

MESH = pl.DeviceIdType.MESH
F32 = jnp.float32
FIELDS = 5
MODES_HERE = 4
ROWS = 40
DEPTH = 128
SMOOTH = 0.8 / 6.0


def tables(circ, cells):
    total = circ * cells
    sector = np.arange(circ)[:, None]
    position = np.zeros((circ, ROWS), np.int64)
    position[:, :cells] = sector * cells + np.arange(cells)[None]
    position[:, cells] = sector[:, 0] * cells + cells
    position[:, cells + 1] = sector[:, 0] * cells - 1
    valid = np.arange(ROWS) < cells + 2
    owner, part, inner = np.meshgrid(np.arange(circ), np.arange(2), np.arange(MODES_HERE), indexing="ij")
    mode = (owner * MODES_HERE + inner).reshape(-1)
    part = part.reshape(-1)
    phase = (mode[None, :, None] * position[:, None, :]) % total
    angle = phase * (2.0 * math.pi / total)
    value = np.where(part[None, :, None] == 0, np.cos(angle), -np.sin(angle)) * math.sqrt(2.0 / total)
    value = np.where(valid[None, None], value, 0.0).astype(np.float32)
    high = value.astype(jnp.bfloat16).astype(np.float32)
    low = (value - high).astype(jnp.bfloat16).astype(np.float32)
    rest = np.zeros((circ, value.shape[1], DEPTH - 3 * ROWS), np.float32)
    return np.concatenate([high, high, low, rest], axis=2)


def flux(q, w, d, f):
    value = q[f] * w[d]
    if f == 1 + d:
        value = value + w[3]
    if f == 4:
        value = value + w[3] * w[d]
    return value


def primitive(q):
    inverse = 1.0 / q[0]
    u = [q[1 + d] * inverse for d in range(3)]
    p = 0.4 * (q[4] - 0.5 * (q[1] * u[0] + q[2] * u[1] + q[3] * u[2]))
    return u + [p], inverse


def lanes_next(v, lane):
    return jnp.where(lane == 127, v, pltpu.roll(v, 127, 1))


def lanes_prev(v, lane):
    return jnp.where(lane == 0, v, pltpu.roll(v, 1, 1))


def comm_kernel(
    circ, ax,
    st, rot, tab, adv, modes,
    S, W, GA, GC, WG, CS, conv, E, MB, XR, PS, R, MA, RA, MM, RB,
    rotor, load_sem, tab_sem, rot_sem, ga_send, ga_recv, gc_send, gc_recv,
    x_send, x_recv, a_send, a_recv, b_send, b_recv, m_send, m_recv,
):
    r, c, y = lax.axis_index("row"), lax.axis_index("circ"), lax.axis_index("ax")
    na, nt = S.shape[1] - 2, S.shape[2]
    last = ax - 1
    load = pltpu.make_async_copy(st.at[0], S.at[:, pl.ds(1, na)], load_sem)
    load.start()
    table = pltpu.make_async_copy(tab.at[c], E, tab_sem)
    table.start()
    turn = pltpu.make_async_copy(rot, rotor, rot_sem)
    turn.start()

    def near(k):
        return (lax.rem(r + k // ax, 2), c, lax.rem(y + lax.rem(k, ax), ax))

    def far(k):
        return (1 - r, lax.rem(c + k, circ), y)

    right, left = (r, lax.rem(c + 1, circ), y), (r, lax.rem(c + circ - 1, circ), y)
    barrier = pltpu.get_barrier_semaphore()

    def greet(device):
        pl.semaphore_signal(barrier, inc=1, device_id=device, device_id_type=MESH)

    def loop(lo, hi, body):
        def step(i, carry):
            body(i)
            return carry

        lax.fori_loop(lo, hi, step, 0)

    loop(1, 2 * ax, lambda k: greet(near(k)))
    loop(1, circ, lambda k: greet(far(k)))
    greet(right)
    greet(left)

    load.wait()

    def speeds(a, fastest):
        q = [S[f, a] for f in range(FIELDS)]
        w, inverse = primitive(q)
        for i in range(4):
            W[i, a] = w[i]
        speed = jnp.maximum(jnp.maximum(jnp.abs(w[0]), jnp.abs(w[1])), jnp.abs(w[2]))
        speed = speed + jnp.sqrt(1.4 * w[3] * inverse)
        for i in range(nt // 8):
            fastest = jnp.maximum(fastest, speed[8 * i : 8 * i + 8])
        return fastest

    MA[...] = lax.fori_loop(1, na + 1, speeds, jnp.zeros((8, 128), F32))
    for f in range(FIELDS):
        CS[0, f] = S[f, 1 : na + 1, nt - 1]
        CS[1, f] = S[f, 1 : na + 1, 0]

    lane = lax.broadcasted_iota(jnp.int32, (nt, 128), 1)
    cell = lax.broadcasted_iota(jnp.int32, (nt, 128), 0)

    @pl.when(y == last)
    def _():
        q = [S[f, na] for f in range(FIELDS)]
        w = [W[i, na] for i in range(4)]
        qm = [S[f, na - 1] for f in range(FIELDS)]
        wm = [W[i, na - 1] for i in range(4)]
        edge = lax.broadcasted_iota(jnp.int32, (8, 128), 0)
        wide = lax.broadcasted_iota(jnp.int32, (ROWS, 128), 1)

        def inside_next(v):
            return jnp.where(cell == nt - 1, 0.0, pltpu.roll(v, nt - 1, 0))

        def inside_prev(v):
            return jnp.where(cell == 0, 0.0, pltpu.roll(v, 1, 0))

        for f in range(FIELDS):
            qf = q[f]
            smooth = qm[f] - 5.0 * qf + lanes_next(qf, lane) + lanes_prev(qf, lane)
            smooth = smooth + inside_next(qf) + inside_prev(qf)
            still = qf + SMOOTH * smooth
            f1, f2 = flux(q, w, 1, f), flux(q, w, 2, f)
            moved = flux(q, w, 0, f) - flux(qm, wm, 0, f)
            moved = moved + lanes_next(f2, lane) - lanes_prev(f2, lane)
            moved = 0.5 * (moved + inside_next(f1) - inside_prev(f1))
            q_ends = jnp.where(edge == 0, qf[nt - 1 : nt], jnp.where(edge == 1, qf[0:1], 0.0))
            f_ends = jnp.where(edge == 0, -f1[nt - 1 : nt], jnp.where(edge == 1, f1[0:1], 0.0))
            pair = [
                jnp.concatenate([still, SMOOTH * q_ends], axis=0),
                jnp.concatenate([moved, 0.5 * f_ends], axis=0),
            ]
            band = 128 // ax
            for part in range(2):

                def cut(k, carry, part=part, f=f):
                    shift = lax.rem(band * f + 128 - band * k, 128)
                    turned = pltpu.roll(pair[part], shift, 1)
                    if f == 0:
                        MB[k, part] = turned
                    else:
                        MB[k, part] = jnp.where(wide // band == f, turned, MB[k, part])
                    return carry

                lax.fori_loop(0, ax, cut, 0)
        XR[...] = MB[last]

    pl.semaphore_wait(barrier, 2 * ax - 1 + circ - 1 + 2)

    def send(src, dst, sent, got, device):
        return pltpu.make_async_remote_copy(
            src_ref=src, dst_ref=dst, send_sem=sent, recv_sem=got, device_id=device, device_id_type=MESH
        )

    def drain(ref, sem):
        pltpu.make_async_copy(ref, ref, sem).wait()

    loop(1, 2 * ax, lambda k: send(MA, RA.at[k], a_send, a_recv, near(k)).start())

    @pl.when(y == last)
    def _():
        loop(0, last, lambda k: send(MB.at[k], XR, x_send, x_recv, (r, c, k)).start())

    gc_right = send(CS.at[0], GC.at[0], gc_send.at[0], gc_recv.at[0], right)
    gc_left = send(CS.at[1], GC.at[1], gc_send.at[1], gc_recv.at[1], left)
    gc_right.start()
    gc_left.start()
    ga_up = send(S.at[:, na], GA.at[0], ga_send.at[0], ga_recv.at[0], (r, c, lax.rem(y + 1, ax)))
    ga_down = send(S.at[:, 1], GA.at[1], ga_send.at[1], ga_recv.at[1], (r, c, lax.rem(y + last, ax)))
    ga_up.start()
    ga_down.start()

    drain(RA.at[pl.ds(1, 2 * ax - 1)], a_recv)
    MM[...] = lax.fori_loop(1, 2 * ax, lambda k, m: jnp.maximum(m, RA[k]), MA[...])
    loop(1, circ, lambda k: send(MM, RB.at[k], b_send, b_recv, far(k)).start())

    table.wait()

    @pl.when(y != last)
    def _():
        drain(XR, x_recv)

    x = jnp.concatenate([XR[0], XR[1]], axis=1)
    high = x.astype(jnp.bfloat16).astype(F32)
    stack = jnp.concatenate([high, x - high, high, jnp.zeros((DEPTH - 3 * ROWS, 256), F32)], axis=0)
    PS[...] = jnp.dot(E[...].astype(jnp.bfloat16), stack.astype(jnp.bfloat16), preferred_element_type=F32)

    def share(k):
        owner = lax.rem(c + k, circ)
        rows = pl.ds(pl.multiple_of(owner * 8, 8), 8)
        send(PS.at[rows], R.at[k], m_send, m_recv, far(k)).start()

    loop(0, circ, share)

    gc_right.wait_recv()
    gc_left.wait_recv()
    for side in range(2):
        w, _ = primitive([GC[side, f] for f in range(FIELDS)])
        for i in range(4):
            WG[side, i] = w[i]
    ga_up.wait_recv()
    ga_down.wait_recv()
    low_end, high_end = y == 0, y == last
    for f in range(FIELDS):
        S[f, 0] = jnp.where(low_end, S[f, 1], GA[0, f])
        S[f, na + 1] = jnp.where(high_end, S[f, na], GA[1, f])
    for a in (0, na + 1):
        w, _ = primitive([S[f, a] for f in range(FIELDS)])
        for i in range(4):
            W[i, a] = w[i]

    def plane(a, carry):
        q = [S[f, a] for f in range(FIELDS)]
        w = [W[i, a] for i in range(4)]
        row = pl.ds(a - 1, 1)
        gq = [[GC[side, f, row] for f in range(FIELDS)] for side in range(2)]
        gw = [[WG[side, i, row] for i in range(4)] for side in range(2)]
        qu, wu = [S[f, a + 1] for f in range(FIELDS)], [W[i, a + 1] for i in range(4)]
        qd, wd = [S[f, a - 1] for f in range(FIELDS)], [W[i, a - 1] for i in range(4)]
        for f in range(FIELDS):

            def cells_next(v, g):
                return jnp.where(cell == nt - 1, g, pltpu.roll(v, nt - 1, 0))

            def cells_prev(v, g):
                return jnp.where(cell == 0, g, pltpu.roll(v, 1, 0))

            qf = q[f]
            smooth = qu[f] + qd[f] - 6.0 * qf + lanes_next(qf, lane) + lanes_prev(qf, lane)
            smooth = smooth + cells_next(qf, gq[1][f]) + cells_prev(qf, gq[0][f])
            adv[0, f, a - 1] = qf + SMOOTH * smooth
            f1, f2 = flux(q, w, 1, f), flux(q, w, 2, f)
            moved = flux(qu, wu, 0, f) - flux(qd, wd, 0, f)
            moved = moved + lanes_next(f2, lane) - lanes_prev(f2, lane)
            moved = moved + cells_next(f1, flux(gq[1], gw[1], 1, f)) - cells_prev(f1, flux(gq[0], gw[0], 1, f))
            conv[f, a - 1] = 0.5 * moved
        return carry

    lax.fori_loop(1, na + 1, plane, 0)

    turn.wait()
    mode = c * MODES_HERE + lax.rem(lax.broadcasted_iota(jnp.int32, (8, 128), 0), MODES_HERE)
    total = circ * nt
    angle = ((mode * rotor[0, 0]) & (total - 1)).astype(F32) * (2.0 * math.pi / total)
    imaginary = lax.broadcasted_iota(jnp.int32, (8, 128), 0) >= MODES_HERE
    orient = (2 * r - 1).astype(F32)
    cosine = jnp.cos(angle)
    sine = jnp.where(imaginary, orient, -orient) * jnp.sin(angle)

    drain(RB.at[pl.ds(1, circ - 1)], b_recv)
    fastest = lax.fori_loop(1, circ, lambda k, m: jnp.maximum(m, RB[k]), MM[...])
    step = 0.8 / (3.0 * jnp.full((8, 128), jnp.max(fastest), F32))
    step_plane = jnp.concatenate([step] * (nt // 8), axis=0)

    def finish(a):
        for f in range(FIELDS):
            adv[0, f, a] = adv[0, f, a] - step_plane * conv[f, a]

    loop(0, na, finish)

    drain(R, m_recv)
    sums = lax.fori_loop(0, circ, lambda k, s: s + R[k], jnp.zeros((8, 256), F32))
    own = sums[:, :128] - step * sums[:, 128:]
    modes[...] = own * cosine + pltpu.roll(own, MODES_HERE, 0) * sine

    drain(RA.at[pl.ds(1, 2 * ax - 1)], a_send)
    drain(RB.at[pl.ds(1, circ - 1)], b_send)
    drain(R, m_send)

    @pl.when(y == last)
    def _():
        drain(MB.at[pl.ds(0, last)], x_send)

    for copy in (gc_right, gc_left, ga_up, ga_down):
        copy.wait_send()


def finish_kernel(adv, turned, out, modes, sem):
    copy = pltpu.make_async_copy(adv, out, sem)
    copy.start()
    value = turned[...]
    band = modes.shape[-1]
    for f in range(FIELDS):
        here = pltpu.roll(value, 128 - band * f, 1) if f else value
        for i in range(MODES_HERE):
            for part in range(2):
                row = part * MODES_HERE + i
                modes[0, i, f, part : part + 1] = here[row : row + 1, :band]
    copy.wait()


def on_device(circ, ax, state, rotor_step):
    na, nt = state.shape[2], state.shape[3]
    table = jnp.asarray(tables(circ, nt))
    hbm = pl.BlockSpec(memory_space=pltpu.HBM)
    vmem = pl.BlockSpec(memory_space=pltpu.VMEM)
    dma = pltpu.SemaphoreType.DMA
    block = (FIELDS, na, nt, 128)
    adv, turned = pl.pallas_call(
        functools.partial(comm_kernel, circ, ax),
        out_shape=[pltpu.VMEM(state.shape, F32), pltpu.VMEM((8, 128), F32)],
        in_specs=[hbm, hbm, hbm],
        out_specs=[vmem, vmem],
        scratch_shapes=[
            pltpu.VMEM((FIELDS, na + 2, nt, 128), F32),
            pltpu.VMEM((4, na + 2, nt, 128), F32),
            pltpu.VMEM((2, FIELDS, nt, 128), F32),
            pltpu.VMEM((2, FIELDS, na, 128), F32),
            pltpu.VMEM((2, 4, na, 128), F32),
            pltpu.VMEM((2, FIELDS, na, 128), F32),
            pltpu.VMEM(block, F32),
            pltpu.VMEM((circ * 8, DEPTH), F32),
            pltpu.VMEM((ax, 2, ROWS, 128), F32),
            pltpu.VMEM((2, ROWS, 128), F32),
            pltpu.VMEM((circ * 8, 256), F32),
            pltpu.VMEM((circ, 8, 256), F32),
            pltpu.VMEM((8, 128), F32),
            pltpu.VMEM((2 * ax, 8, 128), F32),
            pltpu.VMEM((8, 128), F32),
            pltpu.VMEM((circ, 8, 128), F32),
            pltpu.SMEM((1, 1), jnp.int32),
            dma, dma, dma, dma((2,)), dma((2,)), dma((2,)), dma((2,)),
            dma, dma, dma, dma, dma, dma, dma, dma,
        ],
        compiler_params=pltpu.CompilerParams(
            collective_id=0, has_side_effects=True, vmem_limit_bytes=56 * 2**20
        ),
        name="exchange",
    )(state, rotor_step.reshape(1, 1), table)
    return pl.pallas_call(
        finish_kernel,
        out_shape=[
            jax.ShapeDtypeStruct(state.shape, F32),
            jax.ShapeDtypeStruct((1, MODES_HERE, FIELDS, 2, 128 // ax), F32),
        ],
        in_specs=[vmem, vmem],
        out_specs=[hbm, vmem],
        scratch_shapes=[dma],
        name="finish",
    )(adv, turned)


def solution(mesh):
    return jax.shard_map(
        functools.partial(on_device, mesh.shape["circ"], mesh.shape["ax"]),
        mesh=mesh,
        in_specs=(P("row", None, "ax", "circ", None), P()),
        out_specs=(P("row", None, "ax", "circ", None), P("row", "circ", None, None, "ax")),
        check_vma=False,
    )
```

time: 341 us -> 40.4 us (0.12); the launches traced: 336 us -> 40.2 us
  waiting for transfers between devices: 149 us -> 0 us
  blocking collectives: 119 us -> 0 us
  Pallas kernels: 0 us -> 37.3 us
  starting transfers between devices: 28.1 us -> 0 us
  other arithmetic: 15.3 us -> 0 us
  between operations: 16.3 us -> 1.29 us
  local copies, waits for them, and re-layouts: 7.32 us -> 1.65 us
    unnamed x2 -> x0, waiting for transfers between devices: 149 us -> none
    pmax x1 -> x0, blocking collectives: 96.4 us -> none  [on_device(): speed_max = lax.pmax(wave_speed(current), ('row', 'circ', 'ax'))]
    pallas_call x0 -> x2, Pallas kernels: none -> 37.3 us  [the longest x1 34.3 us: on_device(): pl.pallas_call(functools.partial(comm_kernel, circ, ax), out_shape=[pltpu...]
    ppermute x5 -> x0, starting transfers between devices: 28.1 us -> none  [the longest x2 13 us: with_halo(): lax.ppermute(head, axis, [((i + 1) % count, i) for i in range(ends)])]
    psum x1 -> x0, blocking collectives: 22.5 us -> none  [spread(): return lax.psum(jnp.where(mine, shard, jnp.zeros_like(shard)), axis)]
    unnamed x12 -> x0, other arithmetic: 4.89 us -> none
    unnamed x15 -> x4, local copies, waits for them, and re-layouts: 5.45 us -> 1.65 us
    add x2 -> x0, other arithmetic: 3.8 us -> none  [the longest x1 3.79 us: advance(): return state - time_step * convection + courant / 6.0 * smoothing]
  transfers between devices with their start and end apart: 6 -> 0, of which waited for: 1 -> 0; matrix products, arithmetic and copies ran while one was open for 4% -> 0% of each run, Pallas kernels for 0% -> 0%
where the time goes in v1:
time: 40.4 us; the launch traced here: 40.2 us
  Pallas kernels  37.3 us (92%)
  local copies, waits for them, and re-layouts  1.65 us (4%)
  between operations  1.29 us (3%)
    pallas_call x1, Pallas kernels, on_device(): pl.pallas_call(functools.partial(comm_kernel, circ, ax), out_shape=[pltpu...  34.3 us
    pallas_call x1, Pallas kernels, on_device(): pl.pallas_call(finish_kernel, out_shape=[jax.ShapeDtypeStruct(state.shape...  2.99 us
    unnamed x4, local copies, waits for them, and re-layouts  1.65 us

profile of v1, /device:TPU:1, one launch (start us, length us, event | category | flops | bytes accessed | tf_op | source)
XLA Modules:
  0.0 40.2 jit_solution(1154307235180959378)
XLA Ops:
  1.3 34.3 %exchange.1 = (f32[1,5,16,32,128]{4,3,2,1,0:T(8,128)S(1)}, f32[8,128]{1,0:T(8,128)S(1)}) custom-call(f32[1,5,16,32,128]{4,3,2,1,0:T(8,128)} %st.1, s32[1,1]{1,0:T(1,128)} %bitcast.1.rot, f32[32,256,128]{2,1,0:T(8,128)} %constant.2.clone.tab), custom_call_target="tpu_custom_call" | custom-call | tf_op jit(solution)/shard_map/exchange/pallas_call | solution.py:324
  35.6 0.0 copy-start
  35.6 1.1 %copy-done = f32[1,5,16,32,128]{4,3,2,1,0:T(8,128)} copy-done((f32[1,5,16,32,128]{4,3,2,1,0:T(8,128)}, f32[1,5,16,32,128]{4,3,2,1,0:T(8,128)S(1)}, u32[]{:S(2)}) %copy-start) | copy-done | bytes 1310744
  36.7 0.0 copy-start.1
  36.7 0.6 %copy-done.1 = f32[8,128]{1,0:T(8,128)} copy-done((f32[8,128]{1,0:T(8,128)}, f32[8,128]{1,0:T(8,128)S(1)}, u32[]{:S(2)}) %copy-start.1) | copy-done | bytes 4120
  37.2 3.0 %finish.1 = (f32[1,5,16,32,128]{4,3,2,1,0:T(8,128)}, f32[1,4,5,2,16]{4,3,2,1,0:T(2,128)}) custom-call(f32[1,5,16,32,128]{4,3,2,1,0:T(8,128)} %copy-done, f32[8,128]{1,0:T(8,128)} %copy-done.1), custom_call_target="tpu_custom_call" | custom-call | tf_op jit(solution)/shard_map/finish/pallas_call | solution.py:355
Async XLA Ops:
  35.6 1.1 %copy-start = (f32[1,5,16,32,128]{4,3,2,1,0:T(8,128)}, f32[1,5,16,32,128]{4,3,2,1,0:T(8,128)S(1)}, u32[]{:S(2)}) copy-start(f32[1,5,16,32,128]{4,3,2,1,0:T(8,128)S(1)} %get-tuple-element.4.adv) | copy-start | bytes 3932164
  36.7 0.6 %copy-start.1 = (f32[8,128]{1,0:T(8,128)}, f32[8,128]{1,0:T(8,128)S(1)}, u32[]{:S(2)}) copy-start(f32[8,128]{1,0:T(8,128)S(1)} %get-tuple-element.5.turned) | copy-start | bytes 12292

commit v2 on v1

--- a/solution.py
+++ b/solution.py
@@ -16,6 +16,7 @@
 ROWS = 40
 DEPTH = 128
 SMOOTH = 0.8 / 6.0
+EARLY = 0
 
 
 def tables(circ, cells):
@@ -63,10 +64,19 @@
     return jnp.where(lane == 0, v, pltpu.roll(v, 1, 1))
 
 
+def distance(n, d):
+    return min(d, n - d)
+
+
+def offsets(first, second):
+    pairs = [(d, e) for d in range(first) for e in range(second)]
+    return sorted(pairs, key=lambda p: (-distance(first, p[0]) - distance(second, p[1]), p == (0, 0)))
+
+
 def comm_kernel(
-    circ, ax,
+    circ, across, ax,
     st, rot, tab, adv, modes,
-    S, W, GA, GC, WG, CS, conv, E, MB, XR, PS, R, MA, RA, MM, RB,
+    S, W, GA, GC, KG, CS, conv, E, MB, XR, PS, R, MA, RA, MM, RB,
     rotor, load_sem, tab_sem, rot_sem, ga_send, ga_recv, gc_send, gc_recv,
     x_send, x_recv, a_send, a_recv, b_send, b_recv, m_send, m_recv,
 ):
@@ -80,11 +90,22 @@
     turn = pltpu.make_async_copy(rot, rotor, rot_sem)
     turn.start()
 
-    def near(k):
-        return (lax.rem(r + k // ax, 2), c, lax.rem(y + lax.rem(k, ax), ax))
-
-    def far(k):
-        return (1 - r, lax.rem(c + k, circ), y)
+    along = circ // across
+    lines = [lax.rem(y + d, ax) for d in range(ax)]
+    layers = [lax.rem(c // across + d, along) * across for d in range(along)]
+    columns = [lax.rem(lax.rem(c, across) + d, across) for d in range(across)]
+    near_offsets, far_offsets = offsets(ax, 2), offsets(along, across)
+
+    def near(i):
+        d, e = near_offsets[i]
+        return (1 - r if e else r, c, lines[d])
+
+    def sector(i):
+        d, e = far_offsets[i]
+        return layers[d] + columns[e]
+
+    def far(i):
+        return (1 - r, sector(i), y)
 
     right, left = (r, lax.rem(c + 1, circ), y), (r, lax.rem(c + circ - 1, circ), y)
     barrier = pltpu.get_barrier_semaphore()
@@ -99,8 +120,12 @@
 
         lax.fori_loop(lo, hi, step, 0)
 
-    loop(1, 2 * ax, lambda k: greet(near(k)))
-    loop(1, circ, lambda k: greet(far(k)))
+    for i in range(circ // 2):
+        greet(far(i))
+    for i in range(2 * ax - 1):
+        greet(near(i))
+    for i in range(circ // 2, circ - 1):
+        greet(far(i))
     greet(right)
     greet(left)
 
@@ -124,6 +149,34 @@
 
     lane = lax.broadcasted_iota(jnp.int32, (nt, 128), 1)
     cell = lax.broadcasted_iota(jnp.int32, (nt, 128), 0)
+    edge = lax.broadcasted_iota(jnp.int32, (8, 128), 0)
+
+    def inside_next(v):
+        return jnp.where(cell == nt - 1, 0.0, pltpu.roll(v, nt - 1, 0))
+
+    def inside_prev(v):
+        return jnp.where(cell == 0, 0.0, pltpu.roll(v, 1, 0))
+
+    def plane(a):
+        q, w = [S[f, a] for f in range(FIELDS)], [W[i, a] for i in range(4)]
+        qu, wu = [S[f, a + 1] for f in range(FIELDS)], [W[i, a + 1] for i in range(4)]
+        qd, wd = [S[f, a - 1] for f in range(FIELDS)], [W[i, a - 1] for i in range(4)]
+        for f in range(FIELDS):
+            qf = q[f]
+            smooth = qu[f] + qd[f] - 6.0 * qf + lanes_next(qf, lane) + lanes_prev(qf, lane)
+            adv[0, f, a - 1] = qf + SMOOTH * (smooth + inside_next(qf) + inside_prev(qf))
+            f1, f2 = flux(q, w, 1, f), flux(q, w, 2, f)
+            moved = flux(qu, wu, 0, f) - flux(qd, wd, 0, f)
+            moved = moved + lanes_next(f2, lane) - lanes_prev(f2, lane)
+            conv[f, a - 1] = 0.5 * (moved + inside_next(f1) - inside_prev(f1))
+
+    for a in (0, na + 1):
+        for f in range(FIELDS):
+            S[f, a] = jnp.zeros((nt, 128), F32)
+        for i in range(4):
+            W[i, a] = jnp.zeros((nt, 128), F32)
+
+    band = 128 // ax
 
     @pl.when(y == last)
     def _():
@@ -131,15 +184,8 @@
         w = [W[i, na] for i in range(4)]
         qm = [S[f, na - 1] for f in range(FIELDS)]
         wm = [W[i, na - 1] for i in range(4)]
-        edge = lax.broadcasted_iota(jnp.int32, (8, 128), 0)
-        wide = lax.broadcasted_iota(jnp.int32, (ROWS, 128), 1)
-
-        def inside_next(v):
-            return jnp.where(cell == nt - 1, 0.0, pltpu.roll(v, nt - 1, 0))
-
-        def inside_prev(v):
-            return jnp.where(cell == 0, 0.0, pltpu.roll(v, 1, 0))
-
+        group = lax.broadcasted_iota(jnp.int32, (ROWS, 128), 1) // band
+        terms = [[], []]
         for f in range(FIELDS):
             qf = q[f]
             smooth = qm[f] - 5.0 * qf + lanes_next(qf, lane) + lanes_prev(qf, lane)
@@ -151,25 +197,18 @@
             moved = 0.5 * (moved + inside_next(f1) - inside_prev(f1))
             q_ends = jnp.where(edge == 0, qf[nt - 1 : nt], jnp.where(edge == 1, qf[0:1], 0.0))
             f_ends = jnp.where(edge == 0, -f1[nt - 1 : nt], jnp.where(edge == 1, f1[0:1], 0.0))
-            pair = [
-                jnp.concatenate([still, SMOOTH * q_ends], axis=0),
-                jnp.concatenate([moved, 0.5 * f_ends], axis=0),
-            ]
-            band = 128 // ax
+            for part, (inner, ends) in enumerate(((still, SMOOTH * q_ends), (moved, 0.5 * f_ends))):
+                whole = jnp.concatenate([inner, ends], axis=0)
+                terms[part].append(pltpu.roll(whole, band * f, 1) if f else whole)
+        for k in range(ax):
             for part in range(2):
-
-                def cut(k, carry, part=part, f=f):
-                    shift = lax.rem(band * f + 128 - band * k, 128)
-                    turned = pltpu.roll(pair[part], shift, 1)
-                    if f == 0:
-                        MB[k, part] = turned
-                    else:
-                        MB[k, part] = jnp.where(wide // band == f, turned, MB[k, part])
-                    return carry
-
-                lax.fori_loop(0, ax, cut, 0)
+                chosen = terms[part][0]
+                for f in range(1, FIELDS):
+                    chosen = jnp.where(group == (f + k) % ax, terms[part][f], chosen)
+                MB[k, part] = pltpu.roll(chosen, 128 - band * k, 1) if k else chosen
         XR[...] = MB[last]
 
+    loop(1, 1 + EARLY, plane)
     pl.semaphore_wait(barrier, 2 * ax - 1 + circ - 1 + 2)
 
     def send(src, dst, sent, got, device):
@@ -180,11 +219,13 @@
     def drain(ref, sem):
         pltpu.make_async_copy(ref, ref, sem).wait()
 
-    loop(1, 2 * ax, lambda k: send(MA, RA.at[k], a_send, a_recv, near(k)).start())
+    for i in range(2 * ax - 1):
+        send(MA, RA.at[i], a_send, a_recv, near(i)).start()
 
     @pl.when(y == last)
     def _():
-        loop(0, last, lambda k: send(MB.at[k], XR, x_send, x_recv, (r, c, k)).start())
+        for k in sorted(range(last), key=lambda k: -distance(ax, last - k)):
+            send(MB.at[k], XR, x_send, x_recv, (r, c, k)).start()
 
     gc_right = send(CS.at[0], GC.at[0], gc_send.at[0], gc_recv.at[0], right)
     gc_left = send(CS.at[1], GC.at[1], gc_send.at[1], gc_recv.at[1], left)
@@ -195,9 +236,11 @@
     ga_up.start()
     ga_down.start()
 
-    drain(RA.at[pl.ds(1, 2 * ax - 1)], a_recv)
-    MM[...] = lax.fori_loop(1, 2 * ax, lambda k, m: jnp.maximum(m, RA[k]), MA[...])
-    loop(1, circ, lambda k: send(MM, RB.at[k], b_send, b_recv, far(k)).start())
+    loop(1 + EARLY, na + 1, plane)
+    drain(RA.at[pl.ds(0, 2 * ax - 1)], a_recv)
+    MM[...] = lax.fori_loop(0, 2 * ax - 1, lambda i, m: jnp.maximum(m, RA[i]), MA[...])
+    for i in range(circ - 1):
+        send(MM, RB.at[i], b_send, b_recv, far(i)).start()
 
     table.wait()
 
@@ -210,58 +253,9 @@
     stack = jnp.concatenate([high, x - high, high, jnp.zeros((DEPTH - 3 * ROWS, 256), F32)], axis=0)
     PS[...] = jnp.dot(E[...].astype(jnp.bfloat16), stack.astype(jnp.bfloat16), preferred_element_type=F32)
 
-    def share(k):
-        owner = lax.rem(c + k, circ)
-        rows = pl.ds(pl.multiple_of(owner * 8, 8), 8)
-        send(PS.at[rows], R.at[k], m_send, m_recv, far(k)).start()
-
-    loop(0, circ, share)
-
-    gc_right.wait_recv()
-    gc_left.wait_recv()
-    for side in range(2):
-        w, _ = primitive([GC[side, f] for f in range(FIELDS)])
-        for i in range(4):
-            WG[side, i] = w[i]
-    ga_up.wait_recv()
-    ga_down.wait_recv()
-    low_end, high_end = y == 0, y == last
-    for f in range(FIELDS):
-        S[f, 0] = jnp.where(low_end, S[f, 1], GA[0, f])
-        S[f, na + 1] = jnp.where(high_end, S[f, na], GA[1, f])
-    for a in (0, na + 1):
-        w, _ = primitive([S[f, a] for f in range(FIELDS)])
-        for i in range(4):
-            W[i, a] = w[i]
-
-    def plane(a, carry):
-        q = [S[f, a] for f in range(FIELDS)]
-        w = [W[i, a] for i in range(4)]
-        row = pl.ds(a - 1, 1)
-        gq = [[GC[side, f, row] for f in range(FIELDS)] for side in range(2)]
-        gw = [[WG[side, i, row] for i in range(4)] for side in range(2)]
-        qu, wu = [S[f, a + 1] for f in range(FIELDS)], [W[i, a + 1] for i in range(4)]
-        qd, wd = [S[f, a - 1] for f in range(FIELDS)], [W[i, a - 1] for i in range(4)]
-        for f in range(FIELDS):
-
-            def cells_next(v, g):
-                return jnp.where(cell == nt - 1, g, pltpu.roll(v, nt - 1, 0))
-
-            def cells_prev(v, g):
-                return jnp.where(cell == 0, g, pltpu.roll(v, 1, 0))
-
-            qf = q[f]
-            smooth = qu[f] + qd[f] - 6.0 * qf + lanes_next(qf, lane) + lanes_prev(qf, lane)
-            smooth = smooth + cells_next(qf, gq[1][f]) + cells_prev(qf, gq[0][f])
-            adv[0, f, a - 1] = qf + SMOOTH * smooth
-            f1, f2 = flux(q, w, 1, f), flux(q, w, 2, f)
-            moved = flux(qu, wu, 0, f) - flux(qd, wd, 0, f)
-            moved = moved + lanes_next(f2, lane) - lanes_prev(f2, lane)
-            moved = moved + cells_next(f1, flux(gq[1], gw[1], 1, f)) - cells_prev(f1, flux(gq[0], gw[0], 1, f))
-            conv[f, a - 1] = 0.5 * moved
-        return carry
-
-    lax.fori_loop(1, na + 1, plane, 0)
+    for i in range(circ):
+        rows = pl.ds(pl.multiple_of(sector(i) * 8, 8), 8)
+        send(PS.at[rows], R.at[i], m_send, m_recv, far(i)).start()
 
     turn.wait()
     mode = c * MODES_HERE + lax.rem(lax.broadcasted_iota(jnp.int32, (8, 128), 0), MODES_HERE)
@@ -272,14 +266,38 @@
     cosine = jnp.cos(angle)
     sine = jnp.where(imaginary, orient, -orient) * jnp.sin(angle)
 
-    drain(RB.at[pl.ds(1, circ - 1)], b_recv)
-    fastest = lax.fori_loop(1, circ, lambda k, m: jnp.maximum(m, RB[k]), MM[...])
+    ga_up.wait_recv()
+    ga_down.wait_recv()
+    for side, a, sign, alone in ((0, 0, -0.5, y == 0), (1, na - 1, 0.5, y == last)):
+        ghost = [jnp.where(alone, S[f, a + 1], GA[side, f]) for f in range(FIELDS)]
+        w, _ = primitive(ghost)
+        for f in range(FIELDS):
+            adv[0, f, a] = adv[0, f, a] + SMOOTH * ghost[f]
+            conv[f, a] = conv[f, a] + sign * flux(ghost, w, 0, f)
+    gc_right.wait_recv()
+    gc_left.wait_recv()
+
+    drain(RB.at[pl.ds(0, circ - 1)], b_recv)
+    fastest = lax.fori_loop(0, circ - 1, lambda i, m: jnp.maximum(m, RB[i]), MM[...])
     step = 0.8 / (3.0 * jnp.full((8, 128), jnp.max(fastest), F32))
     step_plane = jnp.concatenate([step] * (nt // 8), axis=0)
 
+    for side, sign in ((0, 0.5), (1, -0.5)):
+        ghost = [GC[side, f] for f in range(FIELDS)]
+        w, _ = primitive(ghost)
+        weight = jnp.concatenate([sign * step] * (na // 8), axis=0)
+        for f in range(FIELDS):
+            KG[side, f] = SMOOTH * ghost[f] + weight * flux(ghost, w, 1, f)
+
     def finish(a):
-        for f in range(FIELDS):
-            adv[0, f, a] = adv[0, f, a] - step_plane * conv[f, a]
+        row = pl.ds(a, 1)
+        for f in range(FIELDS):
+            value = adv[0, f, a] - step_plane * conv[f, a]
+            first = jnp.where(edge == 0, KG[0, f, row], 0.0)
+            final = jnp.where(edge == 7, KG[1, f, row], 0.0)
+            adv[0, f, a, 0:8] = value[0:8] + first
+            adv[0, f, a, 8 : nt - 8] = value[8 : nt - 8]
+            adv[0, f, a, nt - 8 : nt] = value[nt - 8 : nt] + final
 
     loop(0, na, finish)
 
@@ -288,8 +306,8 @@
     own = sums[:, :128] - step * sums[:, 128:]
     modes[...] = own * cosine + pltpu.roll(own, MODES_HERE, 0) * sine
 
-    drain(RA.at[pl.ds(1, 2 * ax - 1)], a_send)
-    drain(RB.at[pl.ds(1, circ - 1)], b_send)
+    drain(RA.at[pl.ds(0, 2 * ax - 1)], a_send)
+    drain(RB.at[pl.ds(0, circ - 1)], b_send)
     drain(R, m_send)
 
     @pl.when(y == last)
@@ -300,9 +318,10 @@
         copy.wait_send()
 
 
-def finish_kernel(adv, turned, out, modes, sem):
-    copy = pltpu.make_async_copy(adv, out, sem)
-    copy.start()
+def finish_kernel(adv, turned, out, out_modes, modes, sems):
+    copies = [pltpu.make_async_copy(adv.at[0, f], out.at[0, f], sems.at[f]) for f in range(FIELDS)]
+    for copy in copies:
+        copy.start()
     value = turned[...]
     band = modes.shape[-1]
     for f in range(FIELDS):
@@ -311,7 +330,10 @@
             for part in range(2):
                 row = part * MODES_HERE + i
                 modes[0, i, f, part : part + 1] = here[row : row + 1, :band]
-    copy.wait()
+    copies.append(pltpu.make_async_copy(modes, out_modes, sems.at[FIELDS]))
+    copies[-1].start()
+    for copy in copies:
+        copy.wait()
 
 
 def on_device(circ, ax, state, rotor_step):
@@ -322,7 +344,7 @@
     dma = pltpu.SemaphoreType.DMA
     block = (FIELDS, na, nt, 128)
     adv, turned = pl.pallas_call(
-        functools.partial(comm_kernel, circ, ax),
+        functools.partial(comm_kernel, circ, 4 if circ % 4 == 0 else 1, ax),
         out_shape=[pltpu.VMEM(state.shape, F32), pltpu.VMEM((8, 128), F32)],
         in_specs=[hbm, hbm, hbm],
         out_specs=[vmem, vmem],
@@ -331,7 +353,7 @@
             pltpu.VMEM((4, na + 2, nt, 128), F32),
             pltpu.VMEM((2, FIELDS, nt, 128), F32),
             pltpu.VMEM((2, FIELDS, na, 128), F32),
-            pltpu.VMEM((2, 4, na, 128), F32),
+            pltpu.VMEM((2, FIELDS, na, 128), F32),
             pltpu.VMEM((2, FIELDS, na, 128), F32),
             pltpu.VMEM(block, F32),
             pltpu.VMEM((circ * 8, DEPTH), F32),
@@ -359,10 +381,11 @@
             jax.ShapeDtypeStruct((1, MODES_HERE, FIELDS, 2, 128 // ax), F32),
         ],
         in_specs=[vmem, vmem],
-        out_specs=[hbm, vmem],
-        scratch_shapes=[dma],
+        out_specs=[hbm, hbm],
+        scratch_shapes=[pltpu.VMEM((1, MODES_HERE, FIELDS, 2, 128 // ax), F32), dma((FIELDS + 1,))],
+        compiler_params=pltpu.CompilerParams(vmem_limit_bytes=16 * 2**20),
         name="finish",
-    )(adv, turned)
+    )(pltpu.with_memory_space_constraint(adv, pltpu.VMEM), pltpu.with_memory_space_constraint(turned, pltpu.VMEM))
 
 
 def solution(mesh):

time: 40.4 us -> 35 us (0.87)
  Pallas kernels: 37.3 us -> 33.5 us
  local copies, waits for them, and re-layouts: 1.65 us -> 0 us
    pallas_call x1, Pallas kernels: 34.3 us -> 32.4 us  [on_device(): pl.pallas_call(functools.partial(comm_kernel, circ, 4 if circ % 4 == 0 el...]
    pallas_call x1, Pallas kernels: 2.99 us -> 1.1 us  [on_device(): pl.pallas_call(finish_kernel, out_shape=[jax.ShapeDtypeStruct(state.shape...]
    unnamed x4 -> x0, local copies, waits for them, and re-layouts: 1.65 us -> none
where the time goes in v2:
time: 35 us; the launch traced here: 34.8 us
  Pallas kernels  33.5 us (96%)
  between operations  1.28 us (4%)
    pallas_call x1, Pallas kernels, on_device(): pl.pallas_call(functools.partial(comm_kernel, circ, 4 if circ % 4 == 0 el...  32.4 us
    pallas_call x1, Pallas kernels, on_device(): pl.pallas_call(finish_kernel, out_shape=[jax.ShapeDtypeStruct(state.shape...  1.1 us

profile of v2, /device:TPU:1, one launch (start us, length us, event | category | flops | bytes accessed | tf_op | source)
XLA Modules:
  0.0 34.8 jit_solution(14269532675157883270)
XLA Ops:
  1.3 32.4 %exchange.1 = (f32[1,5,16,32,128]{4,3,2,1,0:T(8,128)S(1)}, f32[8,128]{1,0:T(8,128)S(1)}) custom-call(f32[1,5,16,32,128]{4,3,2,1,0:T(8,128)} %st.1, s32[1,1]{1,0:T(1,128)} %bitcast.1.rot, f32[32,256,128]{2,1,0:T(8,128)} %constant.2.clone.tab), custom_call_target="tpu_custom_call" | custom-call | tf_op jit(solution)/shard_map/exchange/pallas_call | solution.py:346
  33.7 1.1 %finish.1 = (f32[1,5,16,32,128]{4,3,2,1,0:T(8,128)}, f32[1,4,5,2,16]{4,3,2,1,0:T(2,128)}) custom-call(f32[1,5,16,32,128]{4,3,2,1,0:T(8,128)S(1)} %get-tuple-element.4.adv, f32[8,128]{1,0:T(8,128)S(1)} %get-tuple-element.5.turned), custom_call_target="tpu_custom_call" | custom-call | tf_op jit(solution)/shard_map/finish/pallas_call | solution.py:377

commit v3 on v2

--- a/solution.py
+++ b/solution.py
@@ -15,6 +15,8 @@
 MODES_HERE = 4
 ROWS = 40
 DEPTH = 128
+BAND_ROWS = 48
+SENT = 11
 SMOOTH = 0.8 / 6.0
 EARLY = 0
 
@@ -27,7 +29,7 @@
     position[:, cells] = sector[:, 0] * cells + cells
     position[:, cells + 1] = sector[:, 0] * cells - 1
     valid = np.arange(ROWS) < cells + 2
-    owner, part, inner = np.meshgrid(np.arange(circ), np.arange(2), np.arange(MODES_HERE), indexing="ij")
+    owner, inner, part = np.meshgrid(np.arange(circ), np.arange(MODES_HERE), np.arange(2), indexing="ij")
     mode = (owner * MODES_HERE + inner).reshape(-1)
     part = part.reshape(-1)
     phase = (mode[None, :, None] * position[:, None, :]) % total
@@ -76,9 +78,9 @@
 def comm_kernel(
     circ, across, ax,
     st, rot, tab, adv, modes,
-    S, W, GA, GC, KG, CS, conv, E, MB, XR, PS, R, MA, RA, MM, RB,
+    S, W, GA, GC, KG, CS, conv, E, MB, XR, PS, R, MA, RA, T,
     rotor, load_sem, tab_sem, rot_sem, ga_send, ga_recv, gc_send, gc_recv,
-    x_send, x_recv, a_send, a_recv, b_send, b_recv, m_send, m_recv,
+    x_send, x_recv, a_send, a_recv, m_send, m_recv,
 ):
     r, c, y = lax.axis_index("row"), lax.axis_index("circ"), lax.axis_index("ax")
     na, nt = S.shape[1] - 2, S.shape[2]
@@ -142,7 +144,7 @@
             fastest = jnp.maximum(fastest, speed[8 * i : 8 * i + 8])
         return fastest
 
-    MA[...] = lax.fori_loop(1, na + 1, speeds, jnp.zeros((8, 128), F32))
+    MA[...] = jnp.max(lax.fori_loop(1, na + 1, speeds, jnp.zeros((8, 128), F32)), axis=0, keepdims=True)
     for f in range(FIELDS):
         CS[0, f] = S[f, 1 : na + 1, nt - 1]
         CS[1, f] = S[f, 1 : na + 1, 0]
@@ -185,7 +187,9 @@
         qm = [S[f, na - 1] for f in range(FIELDS)]
         wm = [W[i, na - 1] for i in range(4)]
         group = lax.broadcasted_iota(jnp.int32, (ROWS, 128), 1) // band
+        quarter = group[:8] // 2
         terms = [[], []]
+
         for f in range(FIELDS):
             qf = q[f]
             smooth = qm[f] - 5.0 * qf + lanes_next(qf, lane) + lanes_prev(qf, lane)
@@ -199,13 +203,22 @@
             f_ends = jnp.where(edge == 0, -f1[nt - 1 : nt], jnp.where(edge == 1, f1[0:1], 0.0))
             for part, (inner, ends) in enumerate(((still, SMOOTH * q_ends), (moved, 0.5 * f_ends))):
                 whole = jnp.concatenate([inner, ends], axis=0)
-                terms[part].append(pltpu.roll(whole, band * f, 1) if f else whole)
+                terms[part].append(whole)
+        terms = terms[0] + terms[1]
+        placed = [pltpu.roll(v, band * g, 1) if g else v for g, v in enumerate(terms[:8])]
+        others = [terms[8], pltpu.roll(terms[9], band, 1)]
         for k in range(ax):
-            for part in range(2):
-                chosen = terms[part][0]
-                for f in range(1, FIELDS):
-                    chosen = jnp.where(group == (f + k) % ax, terms[part][f], chosen)
-                MB[k, part] = pltpu.roll(chosen, 128 - band * k, 1) if k else chosen
+            chosen = placed[0]
+            for g in range(1, 8):
+                chosen = jnp.where(group == (g + k) % ax, placed[g], chosen)
+            chosen = pltpu.roll(chosen, 128 - band * k, 1) if k else chosen
+            rest = jnp.where(group == k, others[0], others[1])
+            turned = [pltpu.roll(rest[8 * i : 8 * i + 8], (32 * i - band * k) % 128, 1) for i in range(5)]
+            MB[k, : ROWS - 8] = chosen[: ROWS - 8]
+            MB[k, ROWS - 8 : ROWS] = jnp.where(edge < 2, chosen[ROWS - 8 :], pltpu.roll(turned[4], 2, 0))
+            for i in range(1, 4):
+                turned[0] = jnp.where(quarter == i, turned[i], turned[0])
+            MB[k, ROWS:] = turned[0]
         XR[...] = MB[last]
 
     loop(1, 1 + EARLY, plane)
@@ -219,13 +232,13 @@
     def drain(ref, sem):
         pltpu.make_async_copy(ref, ref, sem).wait()
 
-    for i in range(2 * ax - 1):
-        send(MA, RA.at[i], a_send, a_recv, near(i)).start()
-
     @pl.when(y == last)
     def _():
         for k in sorted(range(last), key=lambda k: -distance(ax, last - k)):
             send(MB.at[k], XR, x_send, x_recv, (r, c, k)).start()
+
+    for i in range(2 * ax - 1):
+        send(MA, RA.at[i], a_send, a_recv, near(i)).start()
 
     gc_right = send(CS.at[0], GC.at[0], gc_send.at[0], gc_recv.at[0], right)
     gc_left = send(CS.at[1], GC.at[1], gc_send.at[1], gc_recv.at[1], left)
@@ -233,14 +246,10 @@
     gc_left.start()
     ga_up = send(S.at[:, na], GA.at[0], ga_send.at[0], ga_recv.at[0], (r, c, lax.rem(y + 1, ax)))
     ga_down = send(S.at[:, 1], GA.at[1], ga_send.at[1], ga_recv.at[1], (r, c, lax.rem(y + last, ax)))
-    ga_up.start()
-    ga_down.start()
 
     loop(1 + EARLY, na + 1, plane)
     drain(RA.at[pl.ds(0, 2 * ax - 1)], a_recv)
-    MM[...] = lax.fori_loop(0, 2 * ax - 1, lambda i, m: jnp.maximum(m, RA[i]), MA[...])
-    for i in range(circ - 1):
-        send(MM, RB.at[i], b_send, b_recv, far(i)).start()
+    fastest = jnp.max(lax.fori_loop(0, 2 * ax - 1, lambda i, m: jnp.maximum(m, RA[i]), MA[...]))
 
     table.wait()
 
@@ -248,20 +257,40 @@
     def _():
         drain(XR, x_recv)
 
-    x = jnp.concatenate([XR[0], XR[1]], axis=1)
-    high = x.astype(jnp.bfloat16).astype(F32)
-    stack = jnp.concatenate([high, x - high, high, jnp.zeros((DEPTH - 3 * ROWS, 256), F32)], axis=0)
-    PS[...] = jnp.dot(E[...].astype(jnp.bfloat16), stack.astype(jnp.bfloat16), preferred_element_type=F32)
+    def split(v):
+        high = v.astype(jnp.bfloat16).astype(F32)
+        parts = [high, v - high, high, jnp.zeros((DEPTH - 3 * ROWS, 128), F32)]
+        return jnp.concatenate(parts, axis=0).astype(jnp.bfloat16)
+
+    packed = XR[ROWS:]
+    rest = [pltpu.roll(packed, 128 - 32 * i, 1) if i else packed for i in range(4)]
+    rest = jnp.concatenate(rest + [pltpu.roll(XR[ROWS - 8 : ROWS], 6, 0)], axis=0)
+    rest = jnp.where(lax.broadcasted_iota(jnp.int32, (ROWS, 128), 1) < 32, rest, 0.0)
+    factors = E[...].reshape(circ, 8, DEPTH)
+
+    def dot(i, v):
+        rows = pltpu.roll(factors, 8 - 2 * i, 1) if i else factors
+        rows = rows.reshape(circ * 8, DEPTH).astype(jnp.bfloat16)
+        return jnp.dot(rows, v, preferred_element_type=F32).reshape(circ, 8, 128)
+
+    PS[:, 0:8] = dot(0, split(XR[:ROWS]))
+    others = dot(0, split(rest))
+    for i in range(1, 4):
+        others = others + dot(i, split(pltpu.roll(rest, 32 * i, 1)))
+    PS[:, 8:16] = jnp.where(lax.broadcasted_iota(jnp.int32, (circ, 8, 128), 1) == 2, fastest, others)
 
     for i in range(circ):
-        rows = pl.ds(pl.multiple_of(sector(i) * 8, 8), 8)
-        send(PS.at[rows], R.at[i], m_send, m_recv, far(i)).start()
+        share = pl.ds(0, SENT)
+        send(PS.at[sector(i), share], R.at[i, share], m_send, m_recv, far(i)).start()
+
+    ga_up.start()
+    ga_down.start()
 
     turn.wait()
-    mode = c * MODES_HERE + lax.rem(lax.broadcasted_iota(jnp.int32, (8, 128), 0), MODES_HERE)
+    mode = c * MODES_HERE + edge // 2
     total = circ * nt
     angle = ((mode * rotor[0, 0]) & (total - 1)).astype(F32) * (2.0 * math.pi / total)
-    imaginary = lax.broadcasted_iota(jnp.int32, (8, 128), 0) >= MODES_HERE
+    imaginary = lax.rem(edge, 2) == 1
     orient = (2 * r - 1).astype(F32)
     cosine = jnp.cos(angle)
     sine = jnp.where(imaginary, orient, -orient) * jnp.sin(angle)
@@ -277,9 +306,17 @@
     gc_right.wait_recv()
     gc_left.wait_recv()
 
-    drain(RB.at[pl.ds(0, circ - 1)], b_recv)
-    fastest = lax.fori_loop(0, circ - 1, lambda i, m: jnp.maximum(m, RB[i]), MM[...])
-    step = 0.8 / (3.0 * jnp.full((8, 128), jnp.max(fastest), F32))
+    drain(R.at[:, pl.ds(0, SENT)], m_recv)
+    speed_row = lax.broadcasted_iota(jnp.int32, (SENT - 8, 128), 0) == 2
+
+    def gather(i, sums):
+        tail = R[i, 8:SENT]
+        return sums[0] + R[i, 0:8], jnp.where(speed_row, jnp.maximum(sums[1], tail), sums[1] + tail)
+
+    sums, tail = lax.fori_loop(1, circ, gather, (R[0, 0:8], R[0, 8:SENT]))
+    T[...] = jnp.zeros((8, 128), F32)
+    T[0 : SENT - 8] = tail
+    step = 0.8 / (3.0 * jnp.full((8, 128), jnp.max(T[2:3]), F32))
     step_plane = jnp.concatenate([step] * (nt // 8), axis=0)
 
     for side, sign in ((0, 0.5), (1, -0.5)):
@@ -300,15 +337,16 @@
             adv[0, f, a, nt - 8 : nt] = value[nt - 8 : nt] + final
 
     loop(0, na, finish)
-
-    drain(R, m_recv)
-    sums = lax.fori_loop(0, circ, lambda k, s: s + R[k], jnp.zeros((8, 256), F32))
-    own = sums[:, :128] - step * sums[:, 128:]
-    modes[...] = own * cosine + pltpu.roll(own, MODES_HERE, 0) * sine
+    moved = pltpu.roll(sums, 128 - band * FIELDS, 1)
+    for i in range(4):
+        piece = pltpu.roll(T[...], (band * 3 - 32 * i) % 128, 1)
+        piece = pltpu.roll(piece, 2 * i, 0) if i else piece
+        moved = jnp.where((edge // 2 == i) & (lane[:8] >= band * 3), piece, moved)
+    own = sums - step * moved
+    modes[...] = own * cosine + jnp.where(imaginary, pltpu.roll(own, 1, 0), pltpu.roll(own, 7, 0)) * sine
 
     drain(RA.at[pl.ds(0, 2 * ax - 1)], a_send)
-    drain(RB.at[pl.ds(0, circ - 1)], b_send)
-    drain(R, m_send)
+    drain(R.at[:, pl.ds(0, SENT)], m_send)
 
     @pl.when(y == last)
     def _():
@@ -328,7 +366,7 @@
         here = pltpu.roll(value, 128 - band * f, 1) if f else value
         for i in range(MODES_HERE):
             for part in range(2):
-                row = part * MODES_HERE + i
+                row = 2 * i + part
                 modes[0, i, f, part : part + 1] = here[row : row + 1, :band]
     copies.append(pltpu.make_async_copy(modes, out_modes, sems.at[FIELDS]))
     copies[-1].start()
@@ -357,17 +395,16 @@
             pltpu.VMEM((2, FIELDS, na, 128), F32),
             pltpu.VMEM(block, F32),
             pltpu.VMEM((circ * 8, DEPTH), F32),
-            pltpu.VMEM((ax, 2, ROWS, 128), F32),
-            pltpu.VMEM((2, ROWS, 128), F32),
-            pltpu.VMEM((circ * 8, 256), F32),
-            pltpu.VMEM((circ, 8, 256), F32),
+            pltpu.VMEM((ax, BAND_ROWS, 128), F32),
+            pltpu.VMEM((BAND_ROWS, 128), F32),
+            pltpu.VMEM((circ, 16, 128), F32),
+            pltpu.VMEM((circ, 16, 128), F32),
+            pltpu.VMEM((1, 128), F32),
+            pltpu.VMEM((2 * ax, 1, 128), F32),
             pltpu.VMEM((8, 128), F32),
-            pltpu.VMEM((2 * ax, 8, 128), F32),
-            pltpu.VMEM((8, 128), F32),
-            pltpu.VMEM((circ, 8, 128), F32),
             pltpu.SMEM((1, 1), jnp.int32),
             dma, dma, dma, dma((2,)), dma((2,)), dma((2,)), dma((2,)),
-            dma, dma, dma, dma, dma, dma, dma, dma,
+            dma, dma, dma, dma, dma, dma,
         ],
         compiler_params=pltpu.CompilerParams(
             collective_id=0, has_side_effects=True, vmem_limit_bytes=56 * 2**20

time: 35 us -> 30.8 us (0.88)
  Pallas kernels: 33.5 us -> 29.4 us
    pallas_call x1, Pallas kernels: 32.4 us -> 28.3 us  [on_device(): pl.pallas_call(functools.partial(comm_kernel, circ, 4 if circ % 4 == 0 el...]
where the time goes in v3:
time: 30.8 us; the launch traced here: 30.7 us
  Pallas kernels  29.4 us (95%)
  between operations  1.28 us (4%)
    pallas_call x1, Pallas kernels, on_device(): pl.pallas_call(functools.partial(comm_kernel, circ, 4 if circ % 4 == 0 el...  28.3 us
    pallas_call x1, Pallas kernels, on_device(): pl.pallas_call(finish_kernel, out_shape=[jax.ShapeDtypeStruct(state.shape...  1.1 us

profile of v3, /device:TPU:1, one launch (start us, length us, event | category | flops | bytes accessed | tf_op | source)
XLA Modules:
  0.0 30.7 jit_solution(2897815284030624890)
XLA Ops:
  1.3 28.3 %exchange.1 = (f32[1,5,16,32,128]{4,3,2,1,0:T(8,128)S(1)}, f32[8,128]{1,0:T(8,128)S(1)}) custom-call(f32[1,5,16,32,128]{4,3,2,1,0:T(8,128)} %st.1, s32[1,1]{1,0:T(1,128)} %bitcast.1.rot, f32[32,256,128]{2,1,0:T(8,128)} %constant.2.clone.tab), custom_call_target="tpu_custom_call" | custom-call | tf_op jit(solution)/shard_map/exchange/pallas_call | solution.py:384
  29.6 1.1 %finish.1 = (f32[1,5,16,32,128]{4,3,2,1,0:T(8,128)}, f32[1,4,5,2,16]{4,3,2,1,0:T(2,128)}) custom-call(f32[1,5,16,32,128]{4,3,2,1,0:T(8,128)S(1)} %get-tuple-element.4.adv, f32[8,128]{1,0:T(8,128)S(1)} %get-tuple-element.5.turned), custom_call_target="tpu_custom_call" | custom-call | tf_op jit(solution)/shard_map/finish/pallas_call | solution.py:414

commit v4 on v3

--- a/solution.py
+++ b/solution.py
@@ -77,8 +77,8 @@
 
 def comm_kernel(
     circ, across, ax,
-    st, rot, tab, adv, modes,
-    S, W, GA, GC, KG, CS, conv, E, MB, XR, PS, R, MA, RA, T,
+    st, rot, tab, base, conv, R, turns,
+    S, W, GA, GC, CS, E, MB, XR, PS, MA, RA,
     rotor, load_sem, tab_sem, rot_sem, ga_send, ga_recv, gc_send, gc_recv,
     x_send, x_recv, a_send, a_recv, m_send, m_recv,
 ):
@@ -166,7 +166,7 @@
         for f in range(FIELDS):
             qf = q[f]
             smooth = qu[f] + qd[f] - 6.0 * qf + lanes_next(qf, lane) + lanes_prev(qf, lane)
-            adv[0, f, a - 1] = qf + SMOOTH * (smooth + inside_next(qf) + inside_prev(qf))
+            base[f, a - 1] = qf + SMOOTH * (smooth + inside_next(qf) + inside_prev(qf))
             f1, f2 = flux(q, w, 1, f), flux(q, w, 2, f)
             moved = flux(qu, wu, 0, f) - flux(qd, wd, 0, f)
             moved = moved + lanes_next(f2, lane) - lanes_prev(f2, lane)
@@ -281,7 +281,7 @@
 
     for i in range(circ):
         share = pl.ds(0, SENT)
-        send(PS.at[sector(i), share], R.at[i, share], m_send, m_recv, far(i)).start()
+        send(PS.at[i, share], R.at[c, share], m_send, m_recv, (1 - r, i, y)).start()
 
     ga_up.start()
     ga_down.start()
@@ -292,8 +292,8 @@
     angle = ((mode * rotor[0, 0]) & (total - 1)).astype(F32) * (2.0 * math.pi / total)
     imaginary = lax.rem(edge, 2) == 1
     orient = (2 * r - 1).astype(F32)
-    cosine = jnp.cos(angle)
-    sine = jnp.where(imaginary, orient, -orient) * jnp.sin(angle)
+    turns[0] = jnp.cos(angle)
+    turns[1] = jnp.where(imaginary, orient, -orient) * jnp.sin(angle)
 
     ga_up.wait_recv()
     ga_down.wait_recv()
@@ -301,67 +301,68 @@
         ghost = [jnp.where(alone, S[f, a + 1], GA[side, f]) for f in range(FIELDS)]
         w, _ = primitive(ghost)
         for f in range(FIELDS):
-            adv[0, f, a] = adv[0, f, a] + SMOOTH * ghost[f]
+            base[f, a] = base[f, a] + SMOOTH * ghost[f]
             conv[f, a] = conv[f, a] + sign * flux(ghost, w, 0, f)
-    gc_right.wait_recv()
-    gc_left.wait_recv()
-
-    drain(R.at[:, pl.ds(0, SENT)], m_recv)
-    speed_row = lax.broadcasted_iota(jnp.int32, (SENT - 8, 128), 0) == 2
-
-    def gather(i, sums):
-        tail = R[i, 8:SENT]
-        return sums[0] + R[i, 0:8], jnp.where(speed_row, jnp.maximum(sums[1], tail), sums[1] + tail)
-
-    sums, tail = lax.fori_loop(1, circ, gather, (R[0, 0:8], R[0, 8:SENT]))
-    T[...] = jnp.zeros((8, 128), F32)
-    T[0 : SENT - 8] = tail
-    step = 0.8 / (3.0 * jnp.full((8, 128), jnp.max(T[2:3]), F32))
-    step_plane = jnp.concatenate([step] * (nt // 8), axis=0)
-
-    for side, sign in ((0, 0.5), (1, -0.5)):
+    for copy in (gc_right, gc_left):
+        copy.wait_send()
+        copy.wait_recv()
+
+    for side, at, row, sign in ((0, 0, 0, -0.5), (1, nt - 8, 7, 0.5)):
         ghost = [GC[side, f] for f in range(FIELDS)]
         w, _ = primitive(ghost)
-        weight = jnp.concatenate([sign * step] * (na // 8), axis=0)
         for f in range(FIELDS):
-            KG[side, f] = SMOOTH * ghost[f] + weight * flux(ghost, w, 1, f)
-
-    def finish(a):
-        row = pl.ds(a, 1)
-        for f in range(FIELDS):
-            value = adv[0, f, a] - step_plane * conv[f, a]
-            first = jnp.where(edge == 0, KG[0, f, row], 0.0)
-            final = jnp.where(edge == 7, KG[1, f, row], 0.0)
-            adv[0, f, a, 0:8] = value[0:8] + first
-            adv[0, f, a, 8 : nt - 8] = value[8 : nt - 8]
-            adv[0, f, a, nt - 8 : nt] = value[nt - 8 : nt] + final
-
-    loop(0, na, finish)
-    moved = pltpu.roll(sums, 128 - band * FIELDS, 1)
-    for i in range(4):
-        piece = pltpu.roll(T[...], (band * 3 - 32 * i) % 128, 1)
-        piece = pltpu.roll(piece, 2 * i, 0) if i else piece
-        moved = jnp.where((edge // 2 == i) & (lane[:8] >= band * 3), piece, moved)
-    own = sums - step * moved
-    modes[...] = own * cosine + jnp.where(imaginary, pltpu.roll(own, 1, 0), pltpu.roll(own, 7, 0)) * sine
+            GC[side, f] = SMOOTH * ghost[f]
+            CS[side, f] = sign * flux(ghost, w, 1, f)
+
+        def ghosts(a, side=side, at=at, row=row):
+            here, rows = pl.ds(a, 1), pl.ds(at, 8)
+            for f in range(FIELDS):
+                base[f, a, rows] = base[f, a, rows] + jnp.where(edge == row, GC[side, f, here], 0.0)
+                conv[f, a, rows] = conv[f, a, rows] + jnp.where(edge == row, CS[side, f, here], 0.0)
+
+        loop(0, na, ghosts)
 
     drain(RA.at[pl.ds(0, 2 * ax - 1)], a_send)
-    drain(R.at[:, pl.ds(0, SENT)], m_send)
 
     @pl.when(y == last)
     def _():
         drain(MB.at[pl.ds(0, last)], x_send)
 
-    for copy in (gc_right, gc_left, ga_up, ga_down):
-        copy.wait_send()
-
-
-def finish_kernel(adv, turned, out, out_modes, modes, sems):
-    copies = [pltpu.make_async_copy(adv.at[0, f], out.at[0, f], sems.at[f]) for f in range(FIELDS)]
-    for copy in copies:
-        copy.start()
-    value = turned[...]
+    ga_up.wait_send()
+    ga_down.wait_send()
+    drain(R.at[:, pl.ds(0, SENT)], m_send)
+    drain(R.at[:, pl.ds(0, SENT)], m_recv)
+
+
+def finish_kernel(base, conv, R, turns, out, out_modes, adv, modes, sems):
+    circ, na, nt = R.shape[0], base.shape[1], base.shape[2]
     band = modes.shape[-1]
+    lane = lax.broadcasted_iota(jnp.int32, (8, 128), 1)
+    edge = lax.broadcasted_iota(jnp.int32, (8, 128), 0)
+
+    fastest = R[0, SENT - 1 : SENT]
+    for i in range(1, circ):
+        fastest = jnp.maximum(fastest, R[i, SENT - 1 : SENT])
+    step = 0.8 / (3.0 * jnp.broadcast_to(fastest, (nt, 128)))
+    copies = []
+    for f in range(FIELDS):
+        for a in range(na):
+            adv[f, a] = base[f, a] - step * conv[f, a]
+        copies.append(pltpu.make_async_copy(adv.at[f], out.at[0, f], sems.at[f]))
+        copies[-1].start()
+
+    sums, tail = R[0, 0:8], R[0, 8 : SENT - 1]
+    for i in range(1, circ):
+        sums, tail = sums + R[i, 0:8], tail + R[i, 8 : SENT - 1]
+    tail = jnp.concatenate([tail, jnp.zeros((17 - SENT, 128), F32)], axis=0)
+    moved = pltpu.roll(sums, 128 - band * FIELDS, 1)
+    for i in range(4):
+        piece = pltpu.roll(tail, (band * 3 - 32 * i) % 128, 1)
+        piece = pltpu.roll(piece, 2 * i, 0) if i else piece
+        moved = jnp.where((edge // 2 == i) & (lane >= band * 3), piece, moved)
+    own = sums - step[:8] * moved
+    other = jnp.where(lax.rem(edge, 2) == 1, pltpu.roll(own, 1, 0), pltpu.roll(own, 7, 0))
+    value = own * turns[0] + other * turns[1]
     for f in range(FIELDS):
         here = pltpu.roll(value, 128 - band * f, 1) if f else value
         for i in range(MODES_HERE):
@@ -381,27 +382,28 @@
     vmem = pl.BlockSpec(memory_space=pltpu.VMEM)
     dma = pltpu.SemaphoreType.DMA
     block = (FIELDS, na, nt, 128)
-    adv, turned = pl.pallas_call(
+    results = pl.pallas_call(
         functools.partial(comm_kernel, circ, 4 if circ % 4 == 0 else 1, ax),
-        out_shape=[pltpu.VMEM(state.shape, F32), pltpu.VMEM((8, 128), F32)],
+        out_shape=[
+            pltpu.VMEM(block, F32),
+            pltpu.VMEM(block, F32),
+            pltpu.VMEM((circ, 16, 128), F32),
+            pltpu.VMEM((2, 8, 128), F32),
+        ],
         in_specs=[hbm, hbm, hbm],
-        out_specs=[vmem, vmem],
+        out_specs=[vmem] * 4,
         scratch_shapes=[
             pltpu.VMEM((FIELDS, na + 2, nt, 128), F32),
             pltpu.VMEM((4, na + 2, nt, 128), F32),
             pltpu.VMEM((2, FIELDS, nt, 128), F32),
             pltpu.VMEM((2, FIELDS, na, 128), F32),
             pltpu.VMEM((2, FIELDS, na, 128), F32),
-            pltpu.VMEM((2, FIELDS, na, 128), F32),
-            pltpu.VMEM(block, F32),
             pltpu.VMEM((circ * 8, DEPTH), F32),
             pltpu.VMEM((ax, BAND_ROWS, 128), F32),
             pltpu.VMEM((BAND_ROWS, 128), F32),
             pltpu.VMEM((circ, 16, 128), F32),
-            pltpu.VMEM((circ, 16, 128), F32),
             pltpu.VMEM((1, 128), F32),
             pltpu.VMEM((2 * ax, 1, 128), F32),
-            pltpu.VMEM((8, 128), F32),
             pltpu.SMEM((1, 1), jnp.int32),
             dma, dma, dma, dma((2,)), dma((2,)), dma((2,)), dma((2,)),
             dma, dma, dma, dma, dma, dma,
@@ -417,12 +419,16 @@
             jax.ShapeDtypeStruct(state.shape, F32),
             jax.ShapeDtypeStruct((1, MODES_HERE, FIELDS, 2, 128 // ax), F32),
         ],
-        in_specs=[vmem, vmem],
+        in_specs=[vmem] * 4,
         out_specs=[hbm, hbm],
-        scratch_shapes=[pltpu.VMEM((1, MODES_HERE, FIELDS, 2, 128 // ax), F32), dma((FIELDS + 1,))],
+        scratch_shapes=[
+            pltpu.VMEM(block, F32),
+            pltpu.VMEM((1, MODES_HERE, FIELDS, 2, 128 // ax), F32),
+            dma((FIELDS + 1,)),
+        ],
         compiler_params=pltpu.CompilerParams(vmem_limit_bytes=16 * 2**20),
         name="finish",
-    )(pltpu.with_memory_space_constraint(adv, pltpu.VMEM), pltpu.with_memory_space_constraint(turned, pltpu.VMEM))
+    )(*(pltpu.with_memory_space_constraint(v, pltpu.VMEM) for v in results))
 
 
 def solution(mesh):

time: 30.8 us -> 29 us (0.942)
  Pallas kernels: 29.4 us -> 27.5 us
    pallas_call x1, Pallas kernels: 28.3 us -> 26.4 us  [on_device(): pl.pallas_call(functools.partial(comm_kernel, circ, 4 if circ % 4 == 0 el...]
where the time goes in v4:
time: 29 us; the launch traced here: 28.8 us
  Pallas kernels  27.5 us (95%)
  between operations  1.28 us (4%)
    pallas_call x1, Pallas kernels, on_device(): pl.pallas_call(functools.partial(comm_kernel, circ, 4 if circ % 4 == 0 el...  26.4 us
    pallas_call x1, Pallas kernels, on_device(): pl.pallas_call(finish_kernel, out_shape=[jax.ShapeDtypeStruct(state.shape...  1.17 us

profile of v4, /device:TPU:1, one launch (start us, length us, event | category | flops | bytes accessed | tf_op | source)
XLA Modules:
  0.0 28.8 jit_solution(148072255224534942)
XLA Ops:
  1.3 26.4 %exchange.1 = (f32[5,16,32,128]{3,2,1,0:T(8,128)S(1)}, f32[5,16,32,128]{3,2,1,0:T(8,128)S(1)}, f32[32,16,128]{2,1,0:T(8,128)S(1)}, f32[2,8,128]{2,1,0:T(8,128)S(1)}) custom-call(f32[1,5,16,32,128]{4,3,2,1,0:T(8,128)} %st.1, s32[1,1]{1,0:T(1,128)} %bitcast.1.rot, f32[32,256,128]{2,1,0:T(8,128)} %constant.2.clone.tab), custom_call_target="tpu_custom_call" | custom-call | tf_op jit(solution)/shard_map/exchange/pallas_call | solution.py:385
  27.6 1.2 %finish.1 = (f32[1,5,16,32,128]{4,3,2,1,0:T(8,128)}, f32[1,4,5,2,16]{4,3,2,1,0:T(2,128)}) custom-call(f32[5,16,32,128]{3,2,1,0:T(8,128)S(1)} %get-tuple-element.6.base, f32[5,16,32,128]{3,2,1,0:T(8,128)S(1)} %get-tuple-element.7.conv, f32[32,16,128]{2,1,0:T(8,128)S(1)} %get-tuple-element.8.R, f32[2,8,128]{2,1,0:T(8,128)S(1)} %get-tuple-element.9.turns), custom_call_target="tpu_custom_call" | custom-call | tf_op jit(solution)/shard_map/finish/pallas_call | solution.py:416

commit v5 on v4

--- a/solution.py
+++ b/solution.py
@@ -18,7 +18,6 @@
 BAND_ROWS = 48
 SENT = 11
 SMOOTH = 0.8 / 6.0
-EARLY = 0
 
 
 def tables(circ, cells):
@@ -78,7 +77,7 @@
 def comm_kernel(
     circ, across, ax,
     st, rot, tab, base, conv, R, turns,
-    S, W, GA, GC, CS, E, MB, XR, PS, MA, RA,
+    S, W, GA, GC, CS, E, EB, MB, XR, PS, MA, RA,
     rotor, load_sem, tab_sem, rot_sem, ga_send, ga_recv, gc_send, gc_recv,
     x_send, x_recv, a_send, a_recv, m_send, m_recv,
 ):
@@ -92,24 +91,12 @@
     turn = pltpu.make_async_copy(rot, rotor, rot_sem)
     turn.start()
 
-    along = circ // across
     lines = [lax.rem(y + d, ax) for d in range(ax)]
-    layers = [lax.rem(c // across + d, along) * across for d in range(along)]
+    near_offsets, far_offsets = offsets(ax, 2), offsets(circ // across, across)[:-1]
+    layers = [lax.rem(c // across + d, circ // across) * across for d in range(circ // across)]
     columns = [lax.rem(lax.rem(c, across) + d, across) for d in range(across)]
-    near_offsets, far_offsets = offsets(ax, 2), offsets(along, across)
-
-    def near(i):
-        d, e = near_offsets[i]
-        return (1 - r if e else r, c, lines[d])
-
-    def sector(i):
-        d, e = far_offsets[i]
-        return layers[d] + columns[e]
-
-    def far(i):
-        return (1 - r, sector(i), y)
-
     right, left = (r, lax.rem(c + 1, circ), y), (r, lax.rem(c + circ - 1, circ), y)
+    up, down = (r, c, lines[1]), (r, c, lines[last])
     barrier = pltpu.get_barrier_semaphore()
 
     def greet(device):
@@ -122,14 +109,19 @@
 
         lax.fori_loop(lo, hi, step, 0)
 
-    for i in range(circ // 2):
-        greet(far(i))
-    for i in range(2 * ax - 1):
-        greet(near(i))
-    for i in range(circ // 2, circ - 1):
-        greet(far(i))
-    greet(right)
-    greet(left)
+    @pl.when(r == 0)
+    def _():
+        for device in (up, down, left, right):
+            greet(device)
+        greet((1, c, y))
+
+    @pl.when(r == 1)
+    def _():
+        for d, e in near_offsets[:-1]:
+            greet((1 - e, c, lines[d]))
+
+    for d, e in far_offsets:
+        greet((1, layers[d] + columns[e], y))
 
     load.wait()
 
@@ -219,10 +211,15 @@
             for i in range(1, 4):
                 turned[0] = jnp.where(quarter == i, turned[i], turned[0])
             MB[k, ROWS:] = turned[0]
-        XR[...] = MB[last]
-
-    loop(1, 1 + EARLY, plane)
-    pl.semaphore_wait(barrier, 2 * ax - 1 + circ - 1 + 2)
+        XR[1] = MB[last]
+
+    @pl.when(r == 0)
+    def _():
+        pl.semaphore_wait(barrier, ax + 4)
+
+    @pl.when(r == 1)
+    def _():
+        pl.semaphore_wait(barrier, ax - 1 + 2 * circ - 1)
 
     def send(src, dst, sent, got, device):
         return pltpu.make_async_remote_copy(
@@ -232,59 +229,113 @@
     def drain(ref, sem):
         pltpu.make_async_copy(ref, ref, sem).wait()
 
+    def band_to(k):
+        return send(MB.at[k], XR.at[r], x_send, x_recv.at[r], (1, c, k))
+
+    by_distance = sorted(range(ax), key=lambda k: -distance(ax, last - k))
+
     @pl.when(y == last)
     def _():
-        for k in sorted(range(last), key=lambda k: -distance(ax, last - k)):
-            send(MB.at[k], XR, x_send, x_recv, (r, c, k)).start()
-
-    for i in range(2 * ax - 1):
-        send(MA, RA.at[i], a_send, a_recv, near(i)).start()
+        for k in by_distance[:-1]:
+            band_to(k).start()
+
+        @pl.when(r == 0)
+        def _():
+            band_to(last).start()
+
+    def speed_to(i):
+        send(MA, RA.at[i], a_send, a_recv, (1, c, lines[near_offsets[i][0]])).start()
+
+    @pl.when(r == 0)
+    def _():
+        for i in range(2 * ax - 1):
+            if near_offsets[i][1]:
+                speed_to(i)
+
+    @pl.when(r == 1)
+    def _():
+        for i in range(2 * ax - 1):
+            if not near_offsets[i][1]:
+                speed_to(i)
 
     gc_right = send(CS.at[0], GC.at[0], gc_send.at[0], gc_recv.at[0], right)
     gc_left = send(CS.at[1], GC.at[1], gc_send.at[1], gc_recv.at[1], left)
     gc_right.start()
     gc_left.start()
-    ga_up = send(S.at[:, na], GA.at[0], ga_send.at[0], ga_recv.at[0], (r, c, lax.rem(y + 1, ax)))
-    ga_down = send(S.at[:, 1], GA.at[1], ga_send.at[1], ga_recv.at[1], (r, c, lax.rem(y + last, ax)))
-
-    loop(1 + EARLY, na + 1, plane)
-    drain(RA.at[pl.ds(0, 2 * ax - 1)], a_recv)
-    fastest = jnp.max(lax.fori_loop(0, 2 * ax - 1, lambda i, m: jnp.maximum(m, RA[i]), MA[...]))
-
+    ga_up = send(S.at[:, na], GA.at[0], ga_send.at[0], ga_recv.at[0], up)
+    ga_down = send(S.at[:, 1], GA.at[1], ga_send.at[1], ga_recv.at[1], down)
+
+    loop(1, na + 1, plane)
     table.wait()
-
-    @pl.when(y != last)
-    def _():
-        drain(XR, x_recv)
+    factors = E[...].reshape(circ, 8, DEPTH)
+    for i in range(4):
+        rows = pltpu.roll(factors, 8 - 2 * i, 1) if i else factors
+        EB[i] = rows.reshape(circ * 8, DEPTH).astype(jnp.bfloat16)
+
+    sent = pl.ds(0, SENT)
 
     def split(v):
         high = v.astype(jnp.bfloat16).astype(F32)
         parts = [high, v - high, high, jnp.zeros((DEPTH - 3 * ROWS, 128), F32)]
         return jnp.concatenate(parts, axis=0).astype(jnp.bfloat16)
 
-    packed = XR[ROWS:]
-    rest = [pltpu.roll(packed, 128 - 32 * i, 1) if i else packed for i in range(4)]
-    rest = jnp.concatenate(rest + [pltpu.roll(XR[ROWS - 8 : ROWS], 6, 0)], axis=0)
-    rest = jnp.where(lax.broadcasted_iota(jnp.int32, (ROWS, 128), 1) < 32, rest, 0.0)
-    factors = E[...].reshape(circ, 8, DEPTH)
-
-    def dot(i, v):
-        rows = pltpu.roll(factors, 8 - 2 * i, 1) if i else factors
-        rows = rows.reshape(circ * 8, DEPTH).astype(jnp.bfloat16)
-        return jnp.dot(rows, v, preferred_element_type=F32).reshape(circ, 8, 128)
-
-    PS[:, 0:8] = dot(0, split(XR[:ROWS]))
-    others = dot(0, split(rest))
-    for i in range(1, 4):
-        others = others + dot(i, split(pltpu.roll(rest, 32 * i, 1)))
-    PS[:, 8:16] = jnp.where(lax.broadcasted_iota(jnp.int32, (circ, 8, 128), 1) == 2, fastest, others)
-
-    for i in range(circ):
-        share = pl.ds(0, SENT)
-        send(PS.at[i, share], R.at[c, share], m_send, m_recv, (1 - r, i, y)).start()
-
-    ga_up.start()
-    ga_down.start()
+    def share(i, source):
+        device, slot = (1 - source, i, y), lax.rem(c - i + circ, circ)
+        return send(PS.at[source, i, sent], R.at[slot, sent], m_send.at[source], m_recv, device)
+
+    @pl.when(r == 1)
+    def _():
+        drain(XR.at[0], x_recv.at[0])
+
+        @pl.when(y != last)
+        def _():
+            drain(XR.at[1], x_recv.at[1])
+
+        ga_up.start()
+        ga_down.start()
+        eight, others = [], []
+        for source in range(2):
+            packed = XR[source, ROWS:]
+            rest = [pltpu.roll(packed, 128 - 32 * i, 1) if i else packed for i in range(4)]
+            rest = jnp.concatenate(rest + [pltpu.roll(XR[source, ROWS - 8 : ROWS], 6, 0)], axis=0)
+            rest = jnp.where(lax.broadcasted_iota(jnp.int32, (ROWS, 128), 1) < 32, rest, 0.0)
+            eight.append(split(XR[source, :ROWS]))
+            others.append([split(pltpu.roll(rest, 32 * i, 1) if i else rest) for i in range(4)])
+
+        def dot(i, v):
+            return jnp.dot(EB[i], v, preferred_element_type=F32).reshape(circ, 8, v.shape[1])
+
+        first = dot(0, jnp.concatenate(eight, axis=1))
+        second = dot(0, jnp.concatenate([others[0][0], others[1][0]], axis=1))
+        for i in range(1, 4):
+            second = second + dot(i, jnp.concatenate([others[0][i], others[1][i]], axis=1))
+        for source in range(2):
+            lanes = slice(128 * source, 128 * source + 128)
+            PS[source, :, 0:8] = first[:, :, lanes]
+            PS[source, :, 8:16] = second[:, :, lanes]
+        drain(RA.at[pl.ds(0, 2 * ax - 1)], a_recv)
+        fastest = MA[...]
+        for i in range(2 * ax - 1):
+            fastest = jnp.maximum(fastest, RA[i])
+        fastest = jnp.full((1, 128), jnp.max(fastest), F32)
+        for source in range(2):
+            for i in range(circ):
+                PS[source, i, SENT - 1 : SENT] = fastest
+
+        for i in range(circ):
+            share(i, 1).start()
+
+            @pl.when(c != i)
+            def _(i=i):
+                share(i, 0).start()
+
+        R[0] = PS[0, c]
+
+    @pl.when(r == 0)
+    def _():
+        ga_up.start()
+        ga_down.start()
+
 
     turn.wait()
     mode = c * MODES_HERE + edge // 2
@@ -322,16 +373,30 @@
 
         loop(0, na, ghosts)
 
-    drain(RA.at[pl.ds(0, 2 * ax - 1)], a_send)
-
-    @pl.when(y == last)
-    def _():
-        drain(MB.at[pl.ds(0, last)], x_send)
-
     ga_up.wait_send()
     ga_down.wait_send()
-    drain(R.at[:, pl.ds(0, SENT)], m_send)
-    drain(R.at[:, pl.ds(0, SENT)], m_recv)
+
+    @pl.when(r == 0)
+    def _():
+        drain(RA.at[pl.ds(0, ax)], a_send)
+
+        @pl.when(y == last)
+        def _():
+            drain(MB, x_send)
+
+        drain(R.at[:, sent], m_recv)
+
+    @pl.when(r == 1)
+    def _():
+        drain(RA.at[pl.ds(0, ax - 1)], a_send)
+
+        @pl.when(y == last)
+        def _():
+            drain(MB.at[pl.ds(0, last)], x_send)
+
+        drain(PS.at[0, pl.ds(1, circ - 1), sent], m_send.at[0])
+        drain(PS.at[1, :, sent], m_send.at[1])
+        drain(R.at[pl.ds(1, circ - 1), sent], m_recv)
 
 
 def finish_kernel(base, conv, R, turns, out, out_modes, adv, modes, sems):
@@ -399,14 +464,15 @@
             pltpu.VMEM((2, FIELDS, na, 128), F32),
             pltpu.VMEM((2, FIELDS, na, 128), F32),
             pltpu.VMEM((circ * 8, DEPTH), F32),
+            pltpu.VMEM((4, circ * 8, DEPTH), jnp.bfloat16),
             pltpu.VMEM((ax, BAND_ROWS, 128), F32),
-            pltpu.VMEM((BAND_ROWS, 128), F32),
-            pltpu.VMEM((circ, 16, 128), F32),
+            pltpu.VMEM((2, BAND_ROWS, 128), F32),
+            pltpu.VMEM((2, circ, 16, 128), F32),
             pltpu.VMEM((1, 128), F32),
             pltpu.VMEM((2 * ax, 1, 128), F32),
             pltpu.SMEM((1, 1), jnp.int32),
             dma, dma, dma, dma((2,)), dma((2,)), dma((2,)), dma((2,)),
-            dma, dma, dma, dma, dma, dma,
+            dma, dma((2,)), dma, dma, dma((2,)), dma,
         ],
         compiler_params=pltpu.CompilerParams(
             collective_id=0, has_side_effects=True, vmem_limit_bytes=56 * 2**20

time: 29 us -> 27.9 us (0.962)
  Pallas kernels: 27.5 us -> 26.5 us
    pallas_call x1, Pallas kernels: 26.4 us -> 25.3 us  [on_device(): pl.pallas_call(functools.partial(comm_kernel, circ, 4 if circ % 4 == 0 el...]
where the time goes in v5:
time: 27.9 us; the launch traced here: 27.7 us
  Pallas kernels  26.5 us (95%)
  between operations  1.28 us (5%)
    pallas_call x1, Pallas kernels, on_device(): pl.pallas_call(functools.partial(comm_kernel, circ, 4 if circ % 4 == 0 el...  25.3 us
    pallas_call x1, Pallas kernels, on_device(): pl.pallas_call(finish_kernel, out_shape=[jax.ShapeDtypeStruct(state.shape...  1.17 us

profile of v5, /device:TPU:1, one launch (start us, length us, event | category | flops | bytes accessed | tf_op | source)
XLA Modules:
  0.0 27.7 jit_solution(16758247730940833339)
XLA Ops:
  1.3 25.3 %exchange.1 = (f32[5,16,32,128]{3,2,1,0:T(8,128)S(1)}, f32[5,16,32,128]{3,2,1,0:T(8,128)S(1)}, f32[32,16,128]{2,1,0:T(8,128)S(1)}, f32[2,8,128]{2,1,0:T(8,128)S(1)}) custom-call(f32[1,5,16,32,128]{4,3,2,1,0:T(8,128)} %st.1, s32[1,1]{1,0:T(1,128)} %bitcast.1.rot, f32[32,256,128]{2,1,0:T(8,128)} %constant.2.clone.tab), custom_call_target="tpu_custom_call" | custom-call | tf_op jit(solution)/shard_map/exchange/pallas_call | solution.py:450
  26.6 1.2 %finish.1 = (f32[1,5,16,32,128]{4,3,2,1,0:T(8,128)}, f32[1,4,5,2,16]{4,3,2,1,0:T(2,128)}) custom-call(f32[5,16,32,128]{3,2,1,0:T(8,128)S(1)} %get-tuple-element.6.base, f32[5,16,32,128]{3,2,1,0:T(8,128)S(1)} %get-tuple-element.7.conv, f32[32,16,128]{2,1,0:T(8,128)S(1)} %get-tuple-element.8.R, f32[2,8,128]{2,1,0:T(8,128)S(1)} %get-tuple-element.9.turns), custom_call_target="tpu_custom_call" | custom-call | tf_op jit(solution)/shard_map/finish/pallas_call | solution.py:482

commit v6 on v5

--- a/solution.py
+++ b/solution.py
@@ -232,7 +232,22 @@
     def band_to(k):
         return send(MB.at[k], XR.at[r], x_send, x_recv.at[r], (1, c, k))
 
-    by_distance = sorted(range(ax), key=lambda k: -distance(ax, last - k))
+    by_distance = sorted(range(ax), key=lambda k: (k == last, distance(ax, k)))
+
+    def speed_to(i):
+        send(MA, RA.at[i], a_send, a_recv, (1, c, lines[near_offsets[i][0]])).start()
+
+    @pl.when(r == 0)
+    def _():
+        for i in range(2 * ax - 1):
+            if near_offsets[i][1]:
+                speed_to(i)
+
+    @pl.when(r == 1)
+    def _():
+        for i in range(2 * ax - 1):
+            if not near_offsets[i][1]:
+                speed_to(i)
 
     @pl.when(y == last)
     def _():
@@ -242,21 +257,6 @@
         @pl.when(r == 0)
         def _():
             band_to(last).start()
-
-    def speed_to(i):
-        send(MA, RA.at[i], a_send, a_recv, (1, c, lines[near_offsets[i][0]])).start()
-
-    @pl.when(r == 0)
-    def _():
-        for i in range(2 * ax - 1):
-            if near_offsets[i][1]:
-                speed_to(i)
-
-    @pl.when(r == 1)
-    def _():
-        for i in range(2 * ax - 1):
-            if not near_offsets[i][1]:
-                speed_to(i)
 
     gc_right = send(CS.at[0], GC.at[0], gc_send.at[0], gc_recv.at[0], right)
     gc_left = send(CS.at[1], GC.at[1], gc_send.at[1], gc_recv.at[1], left)
@@ -322,12 +322,15 @@
             for i in range(circ):
                 PS[source, i, SENT - 1 : SENT] = fastest
 
-        for i in range(circ):
-            share(i, 1).start()
-
-            @pl.when(c != i)
-            def _(i=i):
-                share(i, 0).start()
+        for i in range(0, circ, across):
+            for j in range(i, i + across):
+
+                @pl.when(c != j)
+                def _(j=j):
+                    share(j, 0).start()
+
+            for j in range(i, i + across):
+                share(j, 1).start()
 
         R[0] = PS[0, c]
 

time: 27.9 us -> 27.8 us (level)
  no operation moved by 1% of the time
where the time goes in v6:
time: 27.8 us; the launch traced here: 27.6 us
  Pallas kernels  26.3 us (95%)
  between operations  1.28 us (5%)
    pallas_call x1, Pallas kernels, on_device(): pl.pallas_call(functools.partial(comm_kernel, circ, 4 if circ % 4 == 0 el...  25.2 us
    pallas_call x1, Pallas kernels, on_device(): pl.pallas_call(finish_kernel, out_shape=[jax.ShapeDtypeStruct(state.shape...  1.17 us

profile of v6, /device:TPU:1, one launch (start us, length us, event | category | flops | bytes accessed | tf_op | source)
XLA Modules:
  0.0 27.6 jit_solution(15861722000410375719)
XLA Ops:
  1.3 25.2 %exchange.1 = (f32[5,16,32,128]{3,2,1,0:T(8,128)S(1)}, f32[5,16,32,128]{3,2,1,0:T(8,128)S(1)}, f32[32,16,128]{2,1,0:T(8,128)S(1)}, f32[2,8,128]{2,1,0:T(8,128)S(1)}) custom-call(f32[1,5,16,32,128]{4,3,2,1,0:T(8,128)} %st.1, s32[1,1]{1,0:T(1,128)} %bitcast.1.rot, f32[32,256,128]{2,1,0:T(8,128)} %constant.2.clone.tab), custom_call_target="tpu_custom_call" | custom-call | tf_op jit(solution)/shard_map/exchange/pallas_call | solution.py:453
  26.4 1.2 %finish.1 = (f32[1,5,16,32,128]{4,3,2,1,0:T(8,128)}, f32[1,4,5,2,16]{4,3,2,1,0:T(2,128)}) custom-call(f32[5,16,32,128]{3,2,1,0:T(8,128)S(1)} %get-tuple-element.6.base, f32[5,16,32,128]{3,2,1,0:T(8,128)S(1)} %get-tuple-element.7.conv, f32[32,16,128]{2,1,0:T(8,128)S(1)} %get-tuple-element.8.R, f32[2,8,128]{2,1,0:T(8,128)S(1)} %get-tuple-element.9.turns), custom_call_target="tpu_custom_call" | custom-call | tf_op jit(solution)/shard_map/finish/pallas_call | solution.py:485

commit v7 on v6

--- a/solution.py
+++ b/solution.py
@@ -137,6 +137,42 @@
         return fastest
 
     MA[...] = jnp.max(lax.fori_loop(1, na + 1, speeds, jnp.zeros((8, 128), F32)), axis=0, keepdims=True)
+    @pl.when(r == 0)
+    def _():
+        pl.semaphore_wait(barrier, ax + 4)
+
+    @pl.when(r == 1)
+    def _():
+        pl.semaphore_wait(barrier, ax - 1 + 2 * circ - 1)
+
+    def send(src, dst, sent, got, device):
+        return pltpu.make_async_remote_copy(
+            src_ref=src, dst_ref=dst, send_sem=sent, recv_sem=got, device_id=device, device_id_type=MESH
+        )
+
+    def drain(ref, sem):
+        pltpu.make_async_copy(ref, ref, sem).wait()
+
+    def band_to(k):
+        return send(MB.at[k], XR.at[r], x_send, x_recv.at[r], (1, c, k))
+
+    by_distance = sorted(range(ax), key=lambda k: (k == last, distance(ax, k)))
+
+    def speed_to(i):
+        send(MA, RA.at[i], a_send, a_recv, (1, c, lines[near_offsets[i][0]])).start()
+
+    @pl.when(r == 0)
+    def _():
+        for i in range(2 * ax - 1):
+            if near_offsets[i][1]:
+                speed_to(i)
+
+    @pl.when(r == 1)
+    def _():
+        for i in range(2 * ax - 1):
+            if not near_offsets[i][1]:
+                speed_to(i)
+
     for f in range(FIELDS):
         CS[0, f] = S[f, 1 : na + 1, nt - 1]
         CS[1, f] = S[f, 1 : na + 1, 0]
@@ -213,42 +249,6 @@
             MB[k, ROWS:] = turned[0]
         XR[1] = MB[last]
 
-    @pl.when(r == 0)
-    def _():
-        pl.semaphore_wait(barrier, ax + 4)
-
-    @pl.when(r == 1)
-    def _():
-        pl.semaphore_wait(barrier, ax - 1 + 2 * circ - 1)
-
-    def send(src, dst, sent, got, device):
-        return pltpu.make_async_remote_copy(
-            src_ref=src, dst_ref=dst, send_sem=sent, recv_sem=got, device_id=device, device_id_type=MESH
-        )
-
-    def drain(ref, sem):
-        pltpu.make_async_copy(ref, ref, sem).wait()
-
-    def band_to(k):
-        return send(MB.at[k], XR.at[r], x_send, x_recv.at[r], (1, c, k))
-
-    by_distance = sorted(range(ax), key=lambda k: (k == last, distance(ax, k)))
-
-    def speed_to(i):
-        send(MA, RA.at[i], a_send, a_recv, (1, c, lines[near_offsets[i][0]])).start()
-
-    @pl.when(r == 0)
-    def _():
-        for i in range(2 * ax - 1):
-            if near_offsets[i][1]:
-                speed_to(i)
-
-    @pl.when(r == 1)
-    def _():
-        for i in range(2 * ax - 1):
-            if not near_offsets[i][1]:
-                speed_to(i)
-
     @pl.when(y == last)
     def _():
         for k in by_distance[:-1]:
@@ -265,12 +265,20 @@
     ga_up = send(S.at[:, na], GA.at[0], ga_send.at[0], ga_recv.at[0], up)
     ga_down = send(S.at[:, 1], GA.at[1], ga_send.at[1], ga_recv.at[1], down)
 
+    @pl.when(r == 0)
+    def _():
+        ga_up.start()
+        ga_down.start()
+
     loop(1, na + 1, plane)
     table.wait()
-    factors = E[...].reshape(circ, 8, DEPTH)
-    for i in range(4):
-        rows = pltpu.roll(factors, 8 - 2 * i, 1) if i else factors
-        EB[i] = rows.reshape(circ * 8, DEPTH).astype(jnp.bfloat16)
+
+    @pl.when(r == 1)
+    def _():
+        factors = E[...].reshape(circ, 8, DEPTH)
+        for i in range(4):
+            rows = pltpu.roll(factors, 8 - 2 * i, 1) if i else factors
+            EB[i] = rows.reshape(circ * 8, DEPTH).astype(jnp.bfloat16)
 
     sent = pl.ds(0, SENT)
 
@@ -333,11 +341,6 @@
                 share(j, 1).start()
 
         R[0] = PS[0, c]
-
-    @pl.when(r == 0)
-    def _():
-        ga_up.start()
-        ga_down.start()
 
 
     turn.wait()

time: 27.8 us -> 27.8 us (level)
  no operation moved by 1% of the time
where the time goes in v7:
time: 27.8 us; the launch traced here: 27.6 us
  Pallas kernels  26.3 us (95%)
  between operations  1.28 us (5%)
    pallas_call x1, Pallas kernels, on_device(): pl.pallas_call(functools.partial(comm_kernel, circ, 4 if circ % 4 == 0 el...  25.2 us
    pallas_call x1, Pallas kernels, on_device(): pl.pallas_call(finish_kernel, out_shape=[jax.ShapeDtypeStruct(state.shape...  1.17 us

profile of v7, /device:TPU:1, one launch (start us, length us, event | category | flops | bytes accessed | tf_op | source)
XLA Modules:
  0.0 27.6 jit_solution(17172441824468312250)
XLA Ops:
  1.3 25.2 %exchange.1 = (f32[5,16,32,128]{3,2,1,0:T(8,128)S(1)}, f32[5,16,32,128]{3,2,1,0:T(8,128)S(1)}, f32[32,16,128]{2,1,0:T(8,128)S(1)}, f32[2,8,128]{2,1,0:T(8,128)S(1)}) custom-call(f32[1,5,16,32,128]{4,3,2,1,0:T(8,128)} %st.1, s32[1,1]{1,0:T(1,128)} %bitcast.1.rot, f32[32,256,128]{2,1,0:T(8,128)} %constant.2.clone.tab), custom_call_target="tpu_custom_call" | custom-call | tf_op jit(solution)/shard_map/exchange/pallas_call | solution.py:456
  26.4 1.2 %finish.1 = (f32[1,5,16,32,128]{4,3,2,1,0:T(8,128)}, f32[1,4,5,2,16]{4,3,2,1,0:T(2,128)}) custom-call(f32[5,16,32,128]{3,2,1,0:T(8,128)S(1)} %get-tuple-element.6.base, f32[5,16,32,128]{3,2,1,0:T(8,128)S(1)} %get-tuple-element.7.conv, f32[32,16,128]{2,1,0:T(8,128)S(1)} %get-tuple-element.8.R, f32[2,8,128]{2,1,0:T(8,128)S(1)} %get-tuple-element.9.turns), custom_call_target="tpu_custom_call" | custom-call | tf_op jit(solution)/shard_map/finish/pallas_call | solution.py:488

commit v8 on v6

--- a/solution.py
+++ b/solution.py
@@ -267,10 +267,13 @@
 
     loop(1, na + 1, plane)
     table.wait()
-    factors = E[...].reshape(circ, 8, DEPTH)
-    for i in range(4):
-        rows = pltpu.roll(factors, 8 - 2 * i, 1) if i else factors
-        EB[i] = rows.reshape(circ * 8, DEPTH).astype(jnp.bfloat16)
+
+    @pl.when(r == 1)
+    def _():
+        factors = E[...].reshape(circ, 8, DEPTH)
+        for i in range(4):
+            rows = pltpu.roll(factors, 8 - 2 * i, 1) if i else factors
+            EB[i] = rows.reshape(circ * 8, DEPTH).astype(jnp.bfloat16)
 
     sent = pl.ds(0, SENT)
 

time: 27.8 us -> 27.8 us (level)
  no operation moved by 1% of the time
where the time goes in v8:
time: 27.8 us; the launch traced here: 27.6 us
  Pallas kernels  26.3 us (95%)
  between operations  1.28 us (5%)
    pallas_call x1, Pallas kernels, on_device(): pl.pallas_call(functools.partial(comm_kernel, circ, 4 if circ % 4 == 0 el...  25.2 us
    pallas_call x1, Pallas kernels, on_device(): pl.pallas_call(finish_kernel, out_shape=[jax.ShapeDtypeStruct(state.shape...  1.17 us

profile of v8, /device:TPU:1, one launch (start us, length us, event | category | flops | bytes accessed | tf_op | source)
XLA Modules:
  0.0 27.6 jit_solution(6482912390364411410)
XLA Ops:
  1.3 25.2 %exchange.1 = (f32[5,16,32,128]{3,2,1,0:T(8,128)S(1)}, f32[5,16,32,128]{3,2,1,0:T(8,128)S(1)}, f32[32,16,128]{2,1,0:T(8,128)S(1)}, f32[2,8,128]{2,1,0:T(8,128)S(1)}) custom-call(f32[1,5,16,32,128]{4,3,2,1,0:T(8,128)} %st.1, s32[1,1]{1,0:T(1,128)} %bitcast.1.rot, f32[32,256,128]{2,1,0:T(8,128)} %constant.2.clone.tab), custom_call_target="tpu_custom_call" | custom-call | tf_op jit(solution)/shard_map/exchange/pallas_call | solution.py:456
  26.4 1.2 %finish.1 = (f32[1,5,16,32,128]{4,3,2,1,0:T(8,128)}, f32[1,4,5,2,16]{4,3,2,1,0:T(2,128)}) custom-call(f32[5,16,32,128]{3,2,1,0:T(8,128)S(1)} %get-tuple-element.6.base, f32[5,16,32,128]{3,2,1,0:T(8,128)S(1)} %get-tuple-element.7.conv, f32[32,16,128]{2,1,0:T(8,128)S(1)} %get-tuple-element.8.R, f32[2,8,128]{2,1,0:T(8,128)S(1)} %get-tuple-element.9.turns), custom_call_target="tpu_custom_call" | custom-call | tf_op jit(solution)/shard_map/finish/pallas_call | solution.py:488
